TPU v7x, 512 devices: a whole 4x8x8 slice. The times are simulated.
512 devices in a mesh: wave: 64 (over y, z), lev: 8 (over x, core).
Axes of the slice: x: 4, y: 8, z: 8, core: 2. Of those that a mesh axis runs over, the one named last changes fastest.
Arguments:
- spectral: bfloat16 [820480, 1024], P('wave', 'lev'), may hold values from -0.1796875 to 0.1796875
- table: bfloat16 [32, 820480], P('lev', 'wave'), may hold values from -0.15625 to 0.15625
- wave_owner: int32 [1280], replicated, may hold values from 0 to 63, as said below
- lat_owner: int32 [64], replicated, may hold values from 0 to 63, as said below
- lat_points: int32 [32], replicated, may hold values from 20 to 5136, as said below
Outputs:
- grid: bfloat16 [64, 512, 5376], P('wave', 'lev')
Inputs may be any that keep to these rules, and one draw needn't show every extreme that they name: `wave_owner`: wavenumbers m and 1279 - m have the same owner, and every index of wave owns exactly 10 such pairs. `lat_owner`: every index of wave owns exactly one latitude. `lat_points`: values 20 + 4 i for distinct latitude rows i from 0 to 1279, both ends among them.
All inputs are finite; a program needn't handle non-finite values.
Results may differ from a plain program's by a relative error of at most 0.0055.
Values may be sent and summed in bfloat16 or wider, within the bound.
No kernel may reach another device: no remote copies, remote signals or barrier semaphores. Data moves between devices by JAX's collectives and lax.ppermute only.
A program may use at most 128 MiB of HBM per device.

v0:
```python
import math

import jax
import jax.numpy as jnp
from jax import lax
from jax.sharding import PartitionSpec as P

NLON_PAD = 5376


block_width = 896


def pair_slots(wave_owner, device_count, pairs_per_device):
    pair_count = wave_owner.shape[0] // 2
    owners = wave_owner[:pair_count]
    onehot = (owners[:, None] == jnp.arange(device_count, dtype=jnp.int32)[None, :]).astype(
        jnp.int32
    )
    earlier = jnp.cumsum(onehot, axis=0) - onehot
    position = jnp.sum(earlier * onehot, axis=1)
    global_slot = owners * pairs_per_device + position
    return (
        jnp.zeros((pair_count,), jnp.int32)
        .at[global_slot]
        .set(jnp.arange(pair_count, dtype=jnp.int32))
    )


def per_device(spectral, table, wave_owner, lat_owner, lat_points):
    device_count = lax.axis_size("wave")
    own_index = lax.axis_index("wave")
    wave_count = wave_owner.shape[0]
    trunc_value = wave_count - 1
    pairs_dev = wave_count // (2 * device_count)
    pair_rows = trunc_value + 3
    columns = spectral.shape[1]
    lf_count = columns // 2
    lat_count = lat_owner.shape[0]
    north_count = lat_count // 2
    pair_of_slot = pair_slots(wave_owner, device_count, pairs_dev)
    local_pairs = lax.dynamic_slice_in_dim(pair_of_slot, own_index * pairs_dev, pairs_dev)
    row_index = jnp.arange(pair_rows, dtype=jnp.int32)
    split_row = trunc_value + 1 - local_pairs
    low_mask = row_index[None, :] < split_row[:, None]
    high_mask = jnp.logical_and(
        row_index[None, :] >= split_row[:, None], row_index[None, :] < trunc_value + 2
    )
    blocks = spectral.reshape(pairs_dev, pair_rows, columns)
    zero_value = jnp.zeros((), spectral.dtype)
    halves = jnp.stack(
        [
            jnp.where(low_mask[:, :, None], blocks, zero_value),
            jnp.where(high_mask[:, :, None], blocks, zero_value),
        ],
        axis=1,
    )
    initial = jnp.zeros((pairs_dev, 2, lat_count, columns), jnp.float32)
    low_sign = jnp.broadcast_to((1 - 2 * (row_index % 2))[None, :], (pairs_dev, pair_rows))
    high_sign = 1 - 2 * ((row_index[None, :] + local_pairs[:, None]) % 2)
    signs = jnp.stack([low_sign, high_sign], axis=1).astype(spectral.dtype)
    signed = halves * signs[:, :, :, None]
    carry = initial
    piece = lax.all_gather(table, "lev", axis=0, tiled=True)
    count = piece.shape[0]
    table_view = piece.reshape(count, pairs_dev, pair_rows)
    north = jnp.einsum("kgr,ghrx->ghkx", table_view, halves, preferred_element_type=jnp.float32)
    south = jnp.einsum("kgr,ghrx->ghkx", table_view, signed, preferred_element_type=jnp.float32)
    carry = lax.dynamic_update_slice_in_dim(carry, north, jnp.int32(0), 2)
    four = lax.dynamic_update_slice_in_dim(carry, south, north_count, 2)
    four_slots = four.astype(jnp.bfloat16).reshape(pairs_dev * 2, lat_count, columns)
    holder = (
        jnp.zeros((lat_count,), jnp.int32).at[lat_owner].set(jnp.arange(lat_count, dtype=jnp.int32))
    )
    ordered = jnp.take(four_slots, holder, axis=1)
    received = lax.all_to_all(ordered, "wave", split_axis=1, concat_axis=0, tiled=True)
    coeffs = received.reshape(wave_count, lf_count, 2)
    wave_numbers = jnp.stack([pair_of_slot, trunc_value - pair_of_slot], axis=1).reshape(wave_count)
    my_latitude = holder[own_index]
    points = lat_points[my_latitude % north_count]
    points_float = points.astype(jnp.float32)
    weights = (jnp.where(wave_numbers == 0, 1.0, 2.0) * (2 * wave_numbers < points)).astype(
        jnp.float32
    )
    base_cols = jnp.arange(block_width, dtype=jnp.int32)
    base_phase = wave_numbers[:, None] * base_cols[None, :] % points
    base_angle = 2.0 * math.pi * base_phase.astype(jnp.float32) / points_float
    base_cos = jnp.cos(base_angle)
    base_sin = jnp.sin(base_angle)

    def column_block(index, grid_rows):
        first = index * block_width
        col_index = first + base_cols
        valid = (col_index < points)[None, :]
        turn_phase = wave_numbers * first % points
        turn_angle = 2.0 * math.pi * turn_phase.astype(jnp.float32) / points_float
        turn_cos = jnp.cos(turn_angle)[:, None]
        turn_sin = jnp.sin(turn_angle)[:, None]
        rotated_cos = base_cos * turn_cos - base_sin * turn_sin
        rotated_sin = base_sin * turn_cos + base_cos * turn_sin
        cosine = jnp.where(valid, weights[:, None] * rotated_cos, 0.0)
        sine = jnp.where(valid, -weights[:, None] * rotated_sin, 0.0)
        basis = jnp.stack([cosine, sine], axis=0).astype(jnp.bfloat16)
        values = jnp.einsum("mlc,cmj->lj", coeffs, basis, preferred_element_type=jnp.float32)
        return lax.dynamic_update_slice_in_dim(grid_rows, values, first, 1)

    block_count = NLON_PAD // block_width
    grid_rows = lax.fori_loop(
        0, block_count, column_block, jnp.zeros((lf_count, NLON_PAD), jnp.float32)
    )
    return grid_rows.astype(jnp.bfloat16)[None]


def solution(mesh):
    in_specs = (P("wave", "lev"), P("lev", "wave"), P(), P(), P())
    out_specs = P("wave", "lev", None)
    return jax.shard_map(
        per_device, mesh=mesh, in_specs=in_specs, out_specs=out_specs, check_vma=False
    )
```

profile of v0, /device:TPU:2, one launch (start us, length us, event | category | flops | bytes accessed | tf_op | source)
XLA Modules:
  0.0 502.1 jit_solution(13340638356982381721)
XLA Ops:
  0.7 0.8 scatter_custom_fusion
  1.5 0.7 fusion.72
  2.2 1.5 reduce-window.6
  4.1 0.7 compare_select_fusion.2
  4.8 3.0 reshape.527
  7.8 4.1 scatter_custom_fusion.1
  12.3 17.6 %all-gather = bf16[8,4,12820]{2,1,0:T(4,128)(2,1)} all-gather(bf16[1,4,12820]{2,1,0:T(4,128)(2,1)S(1)} %bitcast.91), channel_id=1, replica_groups=mesh['wave'=64,'lev'=8] {'lev'}, dimensions={0}, use_global_device_ids=true | all-gather | bytes 923040 | tf_op jit(solution)/shard_map/all_gather | solution.py:64
  29.9 3.2 reshape.528
  33.3 5.0 broadcast_select_fusion.1
  38.4 1.4 fusion.44
  39.8 5.4 %fusion.45 = bf16[10,2,128,32]{2,3,1,0:T(8,128)(2,1)S(1)} fusion(bf16[10,1,1282,128]{3,2,1,0:T(8,128)(2,1)S(1)} %get-tuple-element.378, bf16[10,1,1282,128]{3,2,1,0:T(8,128)(2,1)S(1)} %get-tuple-element.377, bf16[10,2,1282]{2,1,0:T(2,128)(2,1)S(1)} %pad_maximum_fusion.6, bf16[32,10,1282,1]{2,1,0,3:T(8,128)(2,1)S(1)} %bitcast.88), kind=kOutput, calls=%fused_computation.53 | convolution fusion | flops 216688640 | bytes 7599440 | tf_op jit(solution)/shard_map/kgr,ghrx->ghkx/dot_general | solution.py:68
  46.1 0.9 select_bitcast_fusion
  47.0 13.8 %all-to-all-start = ((bf16[20,64,128]{2,0,1:T(8,128)(2,1)}), bf16[20,64,128]{2,0,1:T(8,128)(2,1)S(1)}, u32[]{:S(2)}, u32[]{:S(2)}) async-start(bf16[20,64,128]{2,0,1:T(8,128)(2,1)} %select_bitcast_fusion), calls=%async_computation | async-start | bytes 786432 | tf_op jit(solution)/shard_map/all_to_all | solution.py:76
  65.6 0.7 fusion.65
  68.5 9.4 %all-to-all-done = bf16[20,64,128]{2,0,1:T(8,128)(2,1)S(1)} async-done(((bf16[20,64,128]{2,0,1:T(8,128)(2,1)}), bf16[20,64,128]{2,0,1:T(8,128)(2,1)S(1)}, u32[]{:S(2)}, u32[]{:S(2)}) %all-to-all-start) | async-done | bytes 327712 | tf_op jit(solution)/shard_map/all_to_all | solution.py:76
  77.9 3.5 copy.22
  81.4 4.5 reshape.529
  86.0 415.3 %while.17 = (s32[]{:T(128)}, bf16[64,5376]{1,0:T(8,128)(2,1)S(1)}, s32[]{:T(128)}, f32[1280]{0:T(1024)S(1)}, s32[1280]{0:T(1024)S(1)}, /*index=5*/s32[]{:T(128)}...) while((s32[]{:T(128)}, bf16[64,5376]{1,0:T(8,128)(2,1)S(1)}, ...), condition=%wide.region_6.7_spmd.clone.clone, body=%wide.region_5.6_spmd.clone.clone.sunk | while | flops 322289152 | bytes 9785313 | solution.py:108
  86.2 0.7 fusion.83
  86.9 65.7 %fusion.84 = (bf16[1,1280,896]{2,1,0:T(8,128)(2,1)S(1)}, bf16[1,1280,896]{2,1,0:T(8,128)(2,1)}) fusion(f32[1280]{0:T(1024)S(1)} %get-tuple-element.448, f32[1280]{0:T(1024)S(1)} %get-tuple-element.449, f32[1280]{0:T(1024)S(1)} %get-tuple-element.485, f32[]{:T(128)} %get-tuple-element.489, pred[]{:T(512)} %get-tuple-element.488, ...), kind=kLoop, calls=%fused_computation.19.clone.1 | loop fusion | flops 26378240 | bytes 4614025 | tf_op jit(solution)/shard_map/convert
  152.6 2.6 fusion.85
  156.1 65.7 %fusion.84 = (bf16[1,1280,896]{2,1,0:T(8,128)(2,1)S(1)}, bf16[1,1280,896]{2,1,0:T(8,128)(2,1)}) fusion(f32[1280]{0:T(1024)S(1)} %get-tuple-element.448, f32[1280]{0:T(1024)S(1)} %get-tuple-element.449, f32[1280]{0:T(1024)S(1)} %get-tuple-element.485, f32[]{:T(128)} %get-tuple-element.489, pred[]{:T(512)} %get-tuple-element.488, ...), kind=kLoop, calls=%fused_computation.19.clone.1 | loop fusion | flops 26378240 | bytes 4614025 | tf_op jit(solution)/shard_map/convert
  221.8 2.6 fusion.85
  225.3 65.7 %fusion.84 = (bf16[1,1280,896]{2,1,0:T(8,128)(2,1)S(1)}, bf16[1,1280,896]{2,1,0:T(8,128)(2,1)}) fusion(f32[1280]{0:T(1024)S(1)} %get-tuple-element.448, f32[1280]{0:T(1024)S(1)} %get-tuple-element.449, f32[1280]{0:T(1024)S(1)} %get-tuple-element.485, f32[]{:T(128)} %get-tuple-element.489, pred[]{:T(512)} %get-tuple-element.488, ...), kind=kLoop, calls=%fused_computation.19.clone.1 | loop fusion | flops 26378240 | bytes 4614025 | tf_op jit(solution)/shard_map/convert
  291.0 2.6 fusion.85
  294.5 65.7 %fusion.84 = (bf16[1,1280,896]{2,1,0:T(8,128)(2,1)S(1)}, bf16[1,1280,896]{2,1,0:T(8,128)(2,1)}) fusion(f32[1280]{0:T(1024)S(1)} %get-tuple-element.448, f32[1280]{0:T(1024)S(1)} %get-tuple-element.449, f32[1280]{0:T(1024)S(1)} %get-tuple-element.485, f32[]{:T(128)} %get-tuple-element.489, pred[]{:T(512)} %get-tuple-element.488, ...), kind=kLoop, calls=%fused_computation.19.clone.1 | loop fusion | flops 26378240 | bytes 4614025 | tf_op jit(solution)/shard_map/convert
  360.2 2.6 fusion.85
  363.7 65.7 %fusion.84 = (bf16[1,1280,896]{2,1,0:T(8,128)(2,1)S(1)}, bf16[1,1280,896]{2,1,0:T(8,128)(2,1)}) fusion(f32[1280]{0:T(1024)S(1)} %get-tuple-element.448, f32[1280]{0:T(1024)S(1)} %get-tuple-element.449, f32[1280]{0:T(1024)S(1)} %get-tuple-element.485, f32[]{:T(128)} %get-tuple-element.489, pred[]{:T(512)} %get-tuple-element.488, ...), kind=kLoop, calls=%fused_computation.19.clone.1 | loop fusion | flops 26378240 | bytes 4614025 | tf_op jit(solution)/shard_map/convert
  429.4 2.6 fusion.85
  433.0 65.7 %fusion.84 = (bf16[1,1280,896]{2,1,0:T(8,128)(2,1)S(1)}, bf16[1,1280,896]{2,1,0:T(8,128)(2,1)}) fusion(f32[1280]{0:T(1024)S(1)} %get-tuple-element.448, f32[1280]{0:T(1024)S(1)} %get-tuple-element.449, f32[1280]{0:T(1024)S(1)} %get-tuple-element.485, f32[]{:T(128)} %get-tuple-element.489, pred[]{:T(512)} %get-tuple-element.488, ...), kind=kLoop, calls=%fused_computation.19.clone.1 | loop fusion | flops 26378240 | bytes 4614025 | tf_op jit(solution)/shard_map/convert
  498.6 2.6 fusion.85
  501.3 0.8 copy-done.1
  (58 shorter events, 10.2 us)
Async XLA Ops:
  4.8 7.5 %copy-start.2 = (bf16[4,12820]{1,0:T(4,128)(2,1)S(1)}, bf16[4,12820]{1,0:T(4,128)(2,1)}, u32[]{:S(2)}) copy-start(bf16[4,12820]{1,0:T(4,128)(2,1)} %param.8) | copy-start | bytes 307684
  33.3 5.0 copy-start
  45.2 18.3 %copy-start.3 = (s32[32]{0:T(128)S(1)}, s32[32]{0:T(128)}, u32[]{:S(2)}) copy-start(s32[32]{0:T(128)} %param.11) | copy-start | bytes 388
  47.0 30.9 %all-to-all-start = ((bf16[20,64,128]{2,0,1:T(8,128)(2,1)}), bf16[20,64,128]{2,0,1:T(8,128)(2,1)S(1)}, u32[]{:S(2)}, u32[]{:S(2)}) async-start(bf16[20,64,128]{2,0,1:T(8,128)(2,1)} %select_bitcast_fusion), calls=%async_computation | async-start | bytes 786432 | tf_op jit(solution)/shard_map/all_to_all | solution.py:76
  501.3 0.8 copy-start.1
where the time goes:
time: 503 us; the launch traced here: 502 us
  other arithmetic  410 us (82%)
  local copies, waits for them, and re-layouts  23.8 us (5%)
  matrix products  22.6 us (4%)
  blocking collectives  17.6 us (3%)
  starting transfers between devices  13.8 us (3%)
  waiting for transfers between devices  9.42 us (2%)
    another operation x10, other arithmetic  396 us
    all_gather x1, blocking collectives, per_device(): piece = lax.all_gather(table, 'lev', axis=0, tiled=True)  17.6 us
    dot_general x6, matrix products, column_block(): jnp.einsum('mlc,cmj->lj', coeffs, basis, preferred_element_type=jnp.float32)  15.8 us
    all_to_all x1, starting transfers between devices, per_device(): lax.all_to_all(ordered, 'wave', split_axis=1, concat_axis=0, tiled=True)  13.8 us
  transfers between devices with their start and end apart: 1, of which 1 were waited for; matrix products, arithmetic and copies ran while one was open for 1% of the time, Pallas kernels for 0%

commit v1 on v0

v1 whole, which is shorter than its diff:
```python
import functools
import math

import jax
import jax.numpy as jnp
from jax import lax
from jax.experimental import pallas as pl
from jax.experimental.pallas import tpu as pltpu
from jax.sharding import PartitionSpec as P

TRUNC = 1279
PAIRS = 640
PAIRS_DEV = 10
PAIR_ROWS = 1282
ROWS_DEV = 12820
ROWS_PAD = 12928
N_WAVE = 64
NLAT = 64
NORTH = 32
LEVELS = 64
COLS = 128
SLOTS = 20
QUARTER = 1408
NLON_PAD = 5376
LANE = 128

VMEM = pl.BlockSpec(memory_space=pltpu.VMEM)
SMEM = pl.BlockSpec(memory_space=pltpu.SMEM)
f32 = jnp.float32
bf16 = jnp.bfloat16


def iota(shape, dim):
    return lax.broadcasted_iota(jnp.int32, shape, dim)


def to_column(row):
    eye = iota((LANE, LANE), 0) == iota((LANE, LANE), 1)
    parts = []
    for first in range(0, row.shape[1], LANE):
        block = jnp.broadcast_to(row[:, first : first + LANE], (LANE, LANE))
        parts.append(jnp.sum(jnp.where(eye, block, 0.0), axis=1, keepdims=True))
    return jnp.concatenate(parts, axis=0)


def slot_pairs(owner_row):
    owner_col = to_column(owner_row)
    pair_row = iota((1, PAIRS), 1)
    rank = jnp.zeros((1, PAIRS), f32)
    for first in range(0, PAIRS, LANE):
        same = owner_col[first : first + LANE] == owner_row
        earlier = (iota((LANE, PAIRS), 0) + first) < pair_row
        rank += jnp.sum(jnp.where(same & earlier, 1.0, 0.0), axis=0, keepdims=True)
    slot_col = to_column(rank * N_WAVE + owner_row)
    slot_row = iota((1, PAIRS), 1).astype(f32)
    pairs = jnp.zeros((1, PAIRS), f32)
    for first in range(0, PAIRS, LANE):
        here = slot_col[first : first + LANE] == slot_row
        pair = (iota((LANE, PAIRS), 0) + first).astype(f32)
        pairs += jnp.sum(jnp.where(here, pair, 0.0), axis=0, keepdims=True)
    return pairs


def is_odd(value):
    return value - 2.0 * jnp.floor(value * 0.5)


def slots_kernel(me_ref, owner_ref, pairs_ref, local_ref):
    pairs = slot_pairs(owner_ref[...].astype(f32))
    pairs_ref[...] = jnp.broadcast_to(pairs, (8, PAIRS))
    own = iota((16, PAIRS), 0) * N_WAVE + me_ref[0] == iota((16, PAIRS), 1)
    local = jnp.sum(jnp.where(own, pairs, 0.0), axis=1, keepdims=True)
    local_ref[...] = jnp.broadcast_to(local, (16, LANE))


def legendre_kernel(lat_owner_ref, local_ref, table_ref, spectral_ref, out_ref, table, four):
    for index in range(8):
        table[4 * index : 4 * index + 4, 0:ROWS_DEV] = table_ref[index].astype(f32)
    for pair in range(PAIRS_DEV):
        start = PAIR_ROWS * pair // LANE * LANE
        stop = min(-(-PAIR_ROWS * (pair + 1) // LANE) * LANE, ROWS_DEV)
        width = stop - start
        row = (iota((1, width), 1) + (start - PAIR_ROWS * pair)).astype(f32)
        q = local_ref[pair : pair + 1, 0:1]
        q_odd = is_odd(q)
        split = TRUNC + 1 - q
        low = jnp.where((row >= 0) & (row < split), 1.0, 0.0)
        high = jnp.where((row >= split) & (row < TRUNC + 2), 1.0, 0.0)
        even = jnp.where(q_odd > 0, high, low)
        odd = low + high - even
        odd_sign = 1.0 - 2.0 * is_odd(row)
        even_sign = odd_sign * (1.0 - 2.0 * q_odd)
        block = table[:, start:stop]
        left = jnp.concatenate(
            [block * even, block * (even * even_sign), block * odd, block * (odd * odd_sign)], axis=0
        ).astype(bf16)
        values = jnp.dot(left, spectral_ref[start:stop, :], preferred_element_type=f32)
        four[pair * NLAT : (pair + 1) * NLAT, :] = values[:NLAT]
        four[(PAIRS_DEV + pair) * NLAT : (PAIRS_DEV + pair + 1) * NLAT, :] = values[NLAT:]
    for latitude in range(NLAT):
        owner = lat_owner_ref[latitude]
        for part in range(SLOTS // 4):
            rows = four[pl.ds(4 * part * NLAT + latitude, 4, stride=NLAT), :]
            out_ref[owner, part] = rows.astype(bf16)


def circle(quarters_per_turn, numerator, inverse):
    turns = jnp.floor(numerator * inverse + 0.5)
    v = (numerator - turns * quarters_per_turn) * inverse
    z = v * v
    h = math.pi / 2
    sine = v * (h + z * (-(h**3) / 6 + z * (h**5 / 120 + z * (-(h**7) / 5040))))
    cosine = 1.0 + z * (-(h**2) / 2 + z * (h**4 / 24 + z * (-(h**6) / 720 + z * (h**8 / 40320))))
    halves = jnp.floor(turns * 0.5)
    odd_turn = turns - 2.0 * halves
    flip = 1.0 - 2.0 * is_odd(halves)
    swap = odd_turn > 0.5
    out_cos = jnp.where(swap, sine, cosine) * (flip * (1.0 - 2.0 * odd_turn))
    out_sin = jnp.where(swap, cosine, sine) * flip
    return out_cos, -out_sin


def my_points(me_ref, lat_owner_ref, lat_points_ref):
    latitude = jnp.int32(0)
    for index in range(NLAT):
        latitude = jnp.where(lat_owner_ref[index] == me_ref[0], index % NORTH, latitude)
    return lat_points_ref[latitude]


def basis_kernel(me_ref, lat_owner_ref, lat_points_ref, pairs_ref, after_ref, basis_ref, scale_ref, waves):
    del after_ref
    points = my_points(me_ref, lat_owner_ref, lat_points_ref)
    pair = pairs_ref[0:1, :]
    even = jnp.where(is_odd(pair) > 0, TRUNC - pair, pair)
    for index, wave in enumerate((even, TRUNC - even)):
        weight = jnp.where(wave == 0, 1.0, 2.0) * jnp.where(2.0 * wave < points.astype(f32), 1.0, 0.0)
        sign = 1.0 - 2.0 * is_odd(jnp.floor(wave * 0.5))
        scale_ref[2 * index : 2 * index + 1, :] = weight
        scale_ref[2 * index + 1 : 2 * index + 2, :] = weight * sign
        waves[index * PAIRS : (index + 1) * PAIRS, :] = jnp.broadcast_to(to_column(wave), (PAIRS, LANE))
    scale_ref[4:8, :] = jnp.zeros((4, PAIRS), f32)
    quarter = jnp.full((1, LANE), (points // 4).astype(f32))
    inverse = 1.0 / quarter
    step = 32
    column = iota((step, LANE), 1).astype(f32)

    for index in range(2):

        def rows_of(block, carry):
            first = pl.multiple_of(block * step, step)
            wave = waves[pl.ds(index * PAIRS + first, step), :]
            cosine, sine = circle(quarter, wave * column, inverse)
            turn_cos, turn_sin = circle(quarter, wave * float(LANE), inverse)
            for tile in range(QUARTER // LANE):
                at = slice(tile * LANE, (tile + 1) * LANE)
                basis_ref[index, pl.ds(first, step), at] = cosine.astype(bf16)
                basis_ref[index, pl.ds(PAIRS + first, step), at] = sine.astype(bf16)
                cosine, sine = cosine * turn_cos - sine * turn_sin, sine * turn_cos + cosine * turn_sin
            return carry

        lax.fori_loop(0, PAIRS // step, rows_of, 0)


def fourier_kernel(
    me_ref, lat_owner_ref, lat_points_ref, received_ref, scale_ref, basis_ref, out_ref, wide, narrow, left, quarters, grid
):
    points = my_points(me_ref, lat_owner_ref, lat_points_ref)
    quarter = points // 4
    for source in range(N_WAVE):
        for part in range(SLOTS // 4):
            wide[pl.ds(source * 24 + 4 * part, 4), :] = received_ref[source, part].astype(f32)
    for slot in range(SLOTS):
        narrow[slot * N_WAVE : (slot + 1) * N_WAVE, :] = wide[pl.ds(slot, N_WAVE, stride=24), :].astype(bf16)
    out_row, in_col = iota((COLS, COLS), 0), iota((COLS, COLS), 1)
    turn = jnp.where(in_col == 2 * (out_row % LEVELS) + out_row // LEVELS, 1.0, 0.0).astype(bf16)
    for index in range(2):
        turned = lax.dot_general(
            turn,
            narrow[index * PAIRS : (index + 1) * PAIRS, :],
            (((1,), (1,)), ((), ())),
            preferred_element_type=f32,
        )
        weighted = turned * scale_ref[2 * index : 2 * index + 1, :]
        signed = turned * scale_ref[2 * index + 1 : 2 * index + 2, :]
        left[index, :LEVELS, :PAIRS] = weighted[:LEVELS].astype(bf16)
        left[index, :LEVELS, PAIRS:] = weighted[LEVELS:].astype(bf16)
        if index == 0:
            left[index, LEVELS:, :PAIRS] = signed[:LEVELS].astype(bf16)
            left[index, LEVELS:, PAIRS:] = signed[LEVELS:].astype(bf16)
        else:
            left[index, LEVELS:, :PAIRS] = signed[LEVELS:].astype(bf16)
            left[index, LEVELS:, PAIRS:] = -signed[:LEVELS].astype(bf16)
    for first in range(0, QUARTER, 256):
        at = slice(first, min(first + 256, QUARTER))
        even = jnp.dot(left[0], basis_ref[0, :, at], preferred_element_type=f32)
        odd = jnp.dot(left[1], basis_ref[1, :, at], preferred_element_type=f32)
        valid = iota((1, even.shape[1]), 1) + first < quarter
        even = jnp.where(valid, even, 0.0)
        odd = jnp.where(valid, odd, 0.0)
        grid[:, at] = even[:LEVELS] + odd[:LEVELS]
        quarters[0, :, at] = even[LEVELS:] - odd[LEVELS:]
        quarters[1, :, at] = even[:LEVELS] - odd[:LEVELS]
        quarters[2, :, at] = even[LEVELS:] + odd[LEVELS:]
    grid[:, QUARTER:] = jnp.zeros((LEVELS, NLON_PAD - QUARTER), f32)
    lane = iota((LEVELS, LANE), 1)
    for index in range(3):
        offset = (index + 1) * quarter
        base = pl.multiple_of(offset // LANE * LANE, LANE)
        shift = offset - base
        before = jnp.zeros((LEVELS, LANE), f32)
        for tile in range(QUARTER // LANE + 1):
            if tile < QUARTER // LANE:
                now = pltpu.roll(quarters[index, :, tile * LANE : (tile + 1) * LANE], shift, 1)
            else:
                now = jnp.zeros((LEVELS, LANE), f32)
            at = pl.ds(base + tile * LANE, LANE)
            grid[:, at] = grid[:, at] + jnp.where(lane < shift, before, now)
            before = now
    out_ref[0] = grid[...].astype(bf16)


def params(mib):
    return pltpu.CompilerParams(vmem_limit_bytes=mib * 1024 * 1024)


def per_device(spectral, table, wave_owner, lat_owner, lat_points):
    me = lax.axis_index("wave").astype(jnp.int32).reshape(1)
    owner_row = wave_owner[:PAIRS].reshape(1, PAIRS)
    tables = lax.all_gather(table, "lev", axis=0, tiled=False)
    pairs, local = pl.pallas_call(
        slots_kernel,
        out_shape=(jax.ShapeDtypeStruct((8, PAIRS), f32), jax.ShapeDtypeStruct((16, LANE), f32)),
        in_specs=[SMEM, VMEM],
        out_specs=(VMEM, VMEM),
        name="slots",
    )(me, owner_row)
    four = pl.pallas_call(
        legendre_kernel,
        out_shape=jax.ShapeDtypeStruct((N_WAVE, SLOTS // 4, 4, COLS), bf16),
        in_specs=[SMEM, VMEM, VMEM, VMEM],
        out_specs=VMEM,
        scratch_shapes=[pltpu.VMEM((NORTH, ROWS_PAD), f32), pltpu.VMEM((SLOTS * NLAT, COLS), f32)],
        compiler_params=params(32),
        name="legendre",
    )(lat_owner, local, tables, spectral)
    received = lax.all_to_all(four, "wave", split_axis=0, concat_axis=0, tiled=True)
    basis, scale = pl.pallas_call(
        basis_kernel,
        out_shape=(
            jax.ShapeDtypeStruct((2, 2 * PAIRS, QUARTER), bf16),
            jax.ShapeDtypeStruct((8, PAIRS), f32),
        ),
        in_specs=[SMEM, SMEM, SMEM, VMEM, pl.BlockSpec(memory_space=pl.ANY)],
        out_specs=(VMEM, VMEM),
        scratch_shapes=[pltpu.VMEM((2 * PAIRS, LANE), f32)],
        compiler_params=params(24),
        name="basis",
    )(me, lat_owner, lat_points, pairs, four)
    return pl.pallas_call(
        fourier_kernel,
        out_shape=jax.ShapeDtypeStruct((1, LEVELS, NLON_PAD), bf16),
        in_specs=[SMEM, SMEM, SMEM, VMEM, VMEM, VMEM],
        out_specs=VMEM,
        scratch_shapes=[
            pltpu.VMEM((N_WAVE * 24, COLS), f32),
            pltpu.VMEM((SLOTS * N_WAVE, COLS), bf16),
            pltpu.VMEM((2, COLS, 2 * PAIRS), bf16),
            pltpu.VMEM((3, LEVELS, QUARTER), f32),
            pltpu.VMEM((LEVELS, NLON_PAD), f32),
        ],
        compiler_params=params(32),
        name="fourier",
    )(me, lat_owner, lat_points, received, scale, basis)


def solution(mesh):
    in_specs = (P("wave", "lev"), P("lev", "wave"), P(), P(), P())
    out_specs = P("wave", "lev", None)
    return jax.shard_map(
        per_device, mesh=mesh, in_specs=in_specs, out_specs=out_specs, check_vma=False
    )
```

time: 503 us -> 64.5 us (0.13)
  other arithmetic: 410 us -> 0 us
  matrix products: 22.6 us -> 0 us
  Pallas kernels: 0 us -> 13.5 us
  local copies, waits for them, and re-layouts: 23.8 us -> 13.8 us
    another operation x12 -> x0, other arithmetic: 396 us -> none
    dot_general x8 -> x0, matrix products: 22.6 us -> none  [the longest x6 15.8 us: column_block(): jnp.einsum('mlc,cmj->lj', coeffs, basis, preferred_element_type=jnp.float32)]
    pallas_call x0 -> x4, Pallas kernels: none -> 13.5 us  [the longest x1 5.02 us: per_device(): pl.pallas_call(basis_kernel, out_shape=(jax.ShapeDtypeStruct((2, 2 * PAIR...]
    unnamed x9 -> x20, local copies, waits for them, and re-layouts: 0.89 us -> 12.6 us
    reshape x4 -> x1, local copies, waits for them, and re-layouts: 10.8 us -> 0.58 us  [per_device(): owner_row = wave_owner[:PAIRS].reshape(1, PAIRS)]
    select_n x5 -> x0, other arithmetic: 7.23 us -> none  [the longest x1 4.99 us: per_device(): jnp.where(low_mask[:, :, None], blocks, zero_value)]
  transfers between devices with their start and end apart: 1 -> 1, of which waited for: 1 -> 1; matrix products, arithmetic and copies ran while one was open for 1% -> 0% of each run, Pallas kernels for 0% -> 8%
where the time goes in v1:
time: 64.5 us; the launch traced here: 64 us
  blocking collectives  17 us (26%)
  local copies, waits for them, and re-layouts  13.8 us (21%)
  Pallas kernels  13.5 us (21%)
  starting transfers between devices  13.3 us (21%)
  waiting for transfers between devices  6.26 us (10%)
    all_gather x1, blocking collectives, per_device(): tables = lax.all_gather(table, 'lev', axis=0, tiled=False)  17 us
    all_to_all x1, starting transfers between devices, per_device(): lax.all_to_all(four, 'wave', split_axis=0, concat_axis=0, tiled=True)  13.3 us
    unnamed x20, local copies, waits for them, and re-layouts  12.6 us
    all_to_all x1, waiting for transfers between devices, per_device(): lax.all_to_all(four, 'wave', split_axis=0, concat_axis=0, tiled=True)  6.26 us
    pallas_call x1, Pallas kernels, per_device(): pl.pallas_call(basis_kernel, out_shape=(jax.ShapeDtypeStruct((2, 2 * PAIR...  5.02 us
    pallas_call x1, Pallas kernels, per_device(): pl.pallas_call(fourier_kernel, out_shape=jax.ShapeDtypeStruct((1, LEVELS,...  3.35 us
    pallas_call x1, Pallas kernels, per_device(): pl.pallas_call(legendre_kernel, out_shape=jax.ShapeDtypeStruct((N_WAVE, S...  3.17 us
    pallas_call x1, Pallas kernels, per_device(): pl.pallas_call(slots_kernel, out_shape=(jax.ShapeDtypeStruct((8, PAIRS),...  1.99 us
  transfers between devices with their start and end apart: 1, of which 1 were waited for; matrix products, arithmetic and copies ran while one was open for 0% of the time, Pallas kernels for 8%

profile of v1, /device:TPU:2, one launch (start us, length us, event | category | flops | bytes accessed | tf_op | source)
XLA Modules:
  0.0 64.0 jit_solution(9342752529711525030)
XLA Ops:
  0.0 0.7 %slice.3 = s32[640]{0:T(1024)S(1)} slice(s32[1280]{0:T(1024)} %param.7), slice={[0:640]} | slice | bytes 5120 | tf_op jit(solution)/shard_map/slice | solution.py:228
  0.7 0.6 reshape.7.owner_ref
  1.3 17.0 %all-gather.1.table_ref = bf16[8,4,12820]{2,1,0:T(4,128)(2,1)S(1)} all-gather(bf16[1,4,12820]{2,1,0:T(4,128)(2,1)} %bitcast.2), channel_id=2, replica_groups=mesh['wave'=64,'lev'=8] {'lev'}, dimensions={0}, use_global_device_ids=true | all-gather | bytes 923040 | tf_op jit(solution)/shard_map/all_gather | solution.py:229
  18.3 2.0 %slots.1 = (f32[8,640]{1,0:T(8,128)}, f32[16,128]{1,0:T(8,128)}) custom-call(s32[1]{0:T(128)} %bitcast.me_ref, s32[1,640]{1,0:T(1,128)} %reshape.7.owner_ref), custom_call_target="tpu_custom_call" | custom-call | tf_op jit(solution)/shard_map/slots/pallas_call | solution.py:230
  20.3 0.0 copy-start.2
  20.3 1.9 %copy-done.2 = bf16[12820,128]{1,0:T(8,128)(2,1)S(1)} copy-done((bf16[12820,128]{1,0:T(8,128)(2,1)S(1)}, bf16[12820,128]{1,0:T(8,128)(2,1)}, u32[]{:S(2)}) %copy-start.2) | copy-done | bytes 3281944
  22.2 0.0 copy-start.4
  22.2 0.7 %copy-done.4 = f32[16,128]{1,0:T(8,128)S(1)} copy-done((f32[16,128]{1,0:T(8,128)S(1)}, f32[16,128]{1,0:T(8,128)}, u32[]{:S(2)}) %copy-start.4) | copy-done | bytes 8216
  22.9 0.0 copy-start.5
  22.9 0.7 %copy-done.5 = s32[64]{0:T(128)S(1)} copy-done((s32[64]{0:T(128)S(1)}, s32[64]{0:T(128)}, u32[]{:S(2)}) %copy-start.5) | copy-done | bytes 280
  23.6 3.2 %legendre.1.after_ref = bf16[64,5,4,128]{3,2,1,0:T(4,128)(2,1)} custom-call(s32[64]{0:T(128)S(1)} %copy-done.5, f32[16,128]{1,0:T(8,128)S(1)} %copy-done.4, bf16[8,4,12820]{2,1,0:T(4,128)(2,1)S(1)} %all-gather.1.table_ref, bf16[12820,128]{1,0:T(8,128)(2,1)S(1)} %copy-done.2), custom_call_target="tpu_custom_call" | custom-call | tf_op jit(solution)/shard_map/legendre/pallas_call | solution.py:237
  26.7 13.3 %all-to-all-start = ((bf16[64,5,4,128]{3,2,1,0:T(4,128)(2,1)}), bf16[64,5,4,128]{3,2,1,0:T(4,128)(2,1)S(1)}, u32[]{:S(2)}, u32[]{:S(2)}) async-start(bf16[64,5,4,128]{3,2,1,0:T(4,128)(2,1)} %legendre.1.after_ref), calls=%async_computation | async-start | bytes 655360 | tf_op jit(solution)/shard_map/all_to_all | solution.py:246
  40.1 0.0 copy-start.3
  40.1 0.7 %copy-done.3 = f32[8,640]{1,0:T(8,128)S(1)} copy-done((f32[8,640]{1,0:T(8,128)S(1)}, f32[8,640]{1,0:T(8,128)}, u32[]{:S(2)}) %copy-start.3) | copy-done | bytes 20504
  40.8 0.0 copy-start.6
  40.8 0.7 %copy-done.6 = s32[64]{0:T(128)S(1)} copy-done((s32[64]{0:T(128)S(1)}, s32[64]{0:T(128)}, u32[]{:S(2)}) %copy-start.6) | copy-done | bytes 280
  41.5 0.0 copy-start.8
  41.5 0.7 %copy-done.8 = s32[32]{0:T(128)S(1)} copy-done((s32[32]{0:T(128)S(1)}, s32[32]{0:T(128)}, u32[]{:S(2)}) %copy-start.8) | copy-done | bytes 152
  42.1 5.0 %basis.1 = (bf16[2,1280,1408]{2,1,0:T(8,128)(2,1)S(1)}, f32[8,640]{1,0:T(8,128)S(1)}) custom-call(s32[1]{0:T(128)} %bitcast.me_ref, s32[64]{0:T(128)S(1)} %copy-done.6, s32[32]{0:T(128)S(1)} %copy-done.8, f32[8,640]{1,0:T(8,128)S(1)} %copy-done.3, bf16[64,5,4,128]{3,2,1,0:T(4,128)(2,1)} %legendre.1.after_ref), custom_call_target="tpu_custom_call" | custom-call | tf_op jit(solution)/shard_map/basis/pallas_call | solution.py:247
  47.2 0.0 copy-start
  47.2 2.9 %copy-done = bf16[2,1280,1408]{2,1,0:T(8,128)(2,1)} copy-done((bf16[2,1280,1408]{2,1,0:T(8,128)(2,1)}, bf16[2,1280,1408]{2,1,0:T(8,128)(2,1)S(1)}, u32[]{:S(2)}) %copy-start) | copy-done | bytes 7208984
  50.1 6.3 %all-to-all-done.received_ref = bf16[64,5,4,128]{3,2,1,0:T(4,128)(2,1)S(1)} async-done(((bf16[64,5,4,128]{3,2,1,0:T(4,128)(2,1)}), bf16[64,5,4,128]{3,2,1,0:T(4,128)(2,1)S(1)}, u32[]{:S(2)}, u32[]{:S(2)}) %all-to-all-start) | async-done | bytes 327712 | tf_op jit(solution)/shard_map/all_to_all | solution.py:246
  56.3 0.0 copy-start.1
  56.3 3.0 %copy-done.1 = bf16[2,1280,1408]{2,1,0:T(8,128)(2,1)S(1)} copy-done((bf16[2,1280,1408]{2,1,0:T(8,128)(2,1)S(1)}, bf16[2,1280,1408]{2,1,0:T(8,128)(2,1)}, u32[]{:S(2)}) %copy-start.1) | copy-done | bytes 7208984
  59.4 0.0 copy-start.7
  59.4 0.7 %copy-done.7 = s32[64]{0:T(128)S(1)} copy-done((s32[64]{0:T(128)S(1)}, s32[64]{0:T(128)}, u32[]{:S(2)}) %copy-start.7) | copy-done | bytes 280
  60.0 0.0 copy-start.9
  60.0 0.7 %copy-done.9 = s32[32]{0:T(128)S(1)} copy-done((s32[32]{0:T(128)S(1)}, s32[32]{0:T(128)}, u32[]{:S(2)}) %copy-start.9) | copy-done | bytes 152
  60.7 3.4 %fourier.1 = bf16[1,64,5376]{2,1,0:T(8,128)(2,1)} custom-call(s32[1]{0:T(128)} %bitcast.me_ref, s32[64]{0:T(128)S(1)} %copy-done.7, s32[32]{0:T(128)S(1)} %copy-done.9, bf16[64,5,4,128]{3,2,1,0:T(4,128)(2,1)S(1)} %all-to-all-done.received_ref, f32[8,640]{1,0:T(8,128)S(1)} %get-tuple-element.11.scale_ref, bf16[2,1280,1408]{2,1,0:T(8,128)(2,1)S(1)} %copy-done.1), custom_call_target="tpu_custom_call" | custom-call | tf_op jit(solution)/shard_map/fourier/pallas_call | solution.py:259
Async XLA Ops:
  20.3 1.9 %copy-start.2 = (bf16[12820,128]{1,0:T(8,128)(2,1)S(1)}, bf16[12820,128]{1,0:T(8,128)(2,1)}, u32[]{:S(2)}) copy-start(bf16[12820,128]{1,0:T(8,128)(2,1)} %spectral_ref.1) | copy-start | bytes 9845764
  22.2 0.7 %copy-start.4 = (f32[16,128]{1,0:T(8,128)S(1)}, f32[16,128]{1,0:T(8,128)}, u32[]{:S(2)}) copy-start(f32[16,128]{1,0:T(8,128)} %get-tuple-element.9.local_ref) | copy-start | bytes 24580
  22.9 0.7 %copy-start.5 = (s32[64]{0:T(128)S(1)}, s32[64]{0:T(128)}, u32[]{:S(2)}) copy-start(s32[64]{0:T(128)} %lat_owner_ref.5) | copy-start | bytes 772
  26.7 29.6 %all-to-all-start = ((bf16[64,5,4,128]{3,2,1,0:T(4,128)(2,1)}), bf16[64,5,4,128]{3,2,1,0:T(4,128)(2,1)S(1)}, u32[]{:S(2)}, u32[]{:S(2)}) async-start(bf16[64,5,4,128]{3,2,1,0:T(4,128)(2,1)} %legendre.1.after_ref), calls=%async_computation | async-start | bytes 655360 | tf_op jit(solution)/shard_map/all_to_all | solution.py:246
  40.1 0.7 %copy-start.3 = (f32[8,640]{1,0:T(8,128)S(1)}, f32[8,640]{1,0:T(8,128)}, u32[]{:S(2)}) copy-start(f32[8,640]{1,0:T(8,128)} %get-tuple-element.10.pairs_ref) | copy-start | bytes 61444
  40.8 0.7 %copy-start.6 = (s32[64]{0:T(128)S(1)}, s32[64]{0:T(128)}, u32[]{:S(2)}) copy-start(s32[64]{0:T(128)} %lat_owner_ref.5) | copy-start | bytes 772
  41.5 0.7 %copy-start.8 = (s32[32]{0:T(128)S(1)}, s32[32]{0:T(128)}, u32[]{:S(2)}) copy-start(s32[32]{0:T(128)} %lat_points_ref.3) | copy-start | bytes 388
  47.2 2.9 %copy-start = (bf16[2,1280,1408]{2,1,0:T(8,128)(2,1)}, bf16[2,1280,1408]{2,1,0:T(8,128)(2,1)S(1)}, u32[]{:S(2)}) copy-start(bf16[2,1280,1408]{2,1,0:T(8,128)(2,1)S(1)} %get-tuple-element.12.basis_ref) | copy-start | bytes 21626884
  56.3 3.0 %copy-start.1 = (bf16[2,1280,1408]{2,1,0:T(8,128)(2,1)S(1)}, bf16[2,1280,1408]{2,1,0:T(8,128)(2,1)}, u32[]{:S(2)}) copy-start(bf16[2,1280,1408]{2,1,0:T(8,128)(2,1)} %copy-done) | copy-start | bytes 21626884
  59.4 0.7 %copy-start.7 = (s32[64]{0:T(128)S(1)}, s32[64]{0:T(128)}, u32[]{:S(2)}) copy-start(s32[64]{0:T(128)} %lat_owner_ref.5) | copy-start | bytes 772
  60.0 0.7 %copy-start.9 = (s32[32]{0:T(128)S(1)}, s32[32]{0:T(128)}, u32[]{:S(2)}) copy-start(s32[32]{0:T(128)} %lat_points_ref.3) | copy-start | bytes 388

commit v2 on v1

v2 whole, which is shorter than its diff:
```python
import math

import jax
import jax.numpy as jnp
from jax import lax
from jax.experimental import pallas as pl
from jax.experimental.pallas import tpu as pltpu
from jax.sharding import PartitionSpec as P

TRUNC = 1279
PAIRS = 640
PAIRS_DEV = 10
PAIR_ROWS = 1282
ROWS_DEV = 12820
ROWS_PAD = 12928
N_WAVE = 64
NLAT = 64
NORTH = 32
LEVELS = 64
COLS = 128
SLOTS = 20
QUARTER = 1408
NLON_PAD = 5376
LANE = 128

VMEM = pl.BlockSpec(memory_space=pltpu.VMEM)
SMEM = pl.BlockSpec(memory_space=pltpu.SMEM)
HBM = pl.BlockSpec(memory_space=pltpu.HBM)
f32 = jnp.float32
bf16 = jnp.bfloat16


def iota(shape, dim):
    return lax.broadcasted_iota(jnp.int32, shape, dim)


def to_column(row):
    eye = iota((LANE, LANE), 0) == iota((LANE, LANE), 1)
    parts = []
    for first in range(0, row.shape[1], LANE):
        block = jnp.broadcast_to(row[:, first : first + LANE], (LANE, LANE))
        parts.append(jnp.sum(jnp.where(eye, block, 0.0), axis=1, keepdims=True))
    return jnp.concatenate(parts, axis=0)


def slot_pairs(owner_row):
    owner_col = to_column(owner_row)
    pair_row = iota((1, PAIRS), 1)
    rank = jnp.zeros((1, PAIRS), f32)
    for first in range(0, PAIRS, LANE):
        same = owner_col[first : first + LANE] == owner_row
        earlier = (iota((LANE, PAIRS), 0) + first) < pair_row
        rank += jnp.sum(jnp.where(same & earlier, 1.0, 0.0), axis=0, keepdims=True)
    slot_col = to_column(rank * N_WAVE + owner_row)
    slot_row = iota((1, PAIRS), 1).astype(f32)
    pairs = jnp.zeros((1, PAIRS), f32)
    for first in range(0, PAIRS, LANE):
        here = slot_col[first : first + LANE] == slot_row
        pair = (iota((LANE, PAIRS), 0) + first).astype(f32)
        pairs += jnp.sum(jnp.where(here, pair, 0.0), axis=0, keepdims=True)
    return pairs


def is_odd(value):
    return value - 2.0 * jnp.floor(value * 0.5)


def owner_rows(owner_ref):
    return [owner_ref[pl.ds(first, LANE)].reshape(1, LANE).astype(f32) for first in range(0, PAIRS, LANE)]


def local_pairs(rows, me):
    count = len(rows)
    own = jnp.concatenate([jnp.where(row == me, 1.0, 0.0) for row in rows], axis=0)
    pair = (iota((count, LANE), 0) * LANE + iota((count, LANE), 1)).astype(f32)
    before = jnp.where(iota((LANE, LANE), 0) < iota((LANE, LANE), 1), 1.0, 0.0).astype(bf16)
    rank = jnp.dot(own.astype(bf16), before, preferred_element_type=f32)
    totals = jnp.sum(own, axis=1, keepdims=True)
    carry = jnp.zeros((1, 1), f32)
    carries = []
    for index in range(count):
        carries.append(carry)
        carry = carry + totals[index : index + 1]
    rank = jnp.where(own > 0, rank + jnp.concatenate(carries, axis=0), -1.0)
    return [
        jnp.sum(jnp.sum(jnp.where(rank == index, pair, 0.0), axis=1, keepdims=True), axis=0, keepdims=True)
        for index in range(PAIRS_DEV)
    ]


def first_row(pair):
    return PAIR_ROWS * pair // LANE * LANE


def last_row(pair):
    return min(-(-PAIR_ROWS * (pair + 1) // LANE) * LANE, ROWS_DEV)


def legendre_kernel(
    me_ref, owner_hbm, lat_owner_hbm, table_ref, spectral_hbm, out_ref, owner, lat_owner, table, spectral, four, small, large
):
    copies = [
        pltpu.make_async_copy(owner_hbm, owner, small.at[0]),
        pltpu.make_async_copy(lat_owner_hbm, lat_owner, small.at[1]),
    ]
    pieces = []
    for pair in range(PAIRS_DEV):
        start = last_row(pair - 1) if pair else 0
        at = pl.ds(start, last_row(pair) - start)
        pieces.append(pltpu.make_async_copy(spectral_hbm.at[at], spectral.at[at], large.at[pair]))
    for copy in copies + pieces:
        copy.start()
    for index in range(8):
        table[4 * index : 4 * index + 4, 0:ROWS_DEV] = table_ref[index].astype(f32)
    copies[0].wait()
    locals_ = local_pairs(owner_rows(owner), me_ref[0].astype(f32))
    for pair in range(PAIRS_DEV):
        start, stop = first_row(pair), last_row(pair)
        width = stop - start
        row = (iota((1, width), 1) + (start - PAIR_ROWS * pair)).astype(f32)
        q = locals_[pair]
        q_odd = is_odd(q)
        split = TRUNC + 1 - q
        low = jnp.where((row >= 0) & (row < split), 1.0, 0.0)
        high = jnp.where((row >= split) & (row < TRUNC + 2), 1.0, 0.0)
        even = jnp.where(q_odd > 0, high, low)
        odd = low + high - even
        odd_sign = 1.0 - 2.0 * is_odd(row)
        even_sign = odd_sign * (1.0 - 2.0 * q_odd)
        block = table[:, start:stop]
        left = jnp.concatenate(
            [block * even, block * (even * even_sign), block * odd, block * (odd * odd_sign)], axis=0
        ).astype(bf16)
        if pair in (0, 5):
            for piece in pieces[pair : pair + 5]:
                piece.wait()
        values = jnp.dot(left, spectral[start:stop, :], preferred_element_type=f32)
        four[pair * NLAT : (pair + 1) * NLAT, :] = values[:NLAT]
        four[(PAIRS_DEV + pair) * NLAT : (PAIRS_DEV + pair + 1) * NLAT, :] = values[NLAT:]
    copies[1].wait()
    for latitude in range(NLAT):
        to = lat_owner[latitude]
        for part in range(SLOTS // 4):
            rows = four[pl.ds(4 * part * NLAT + latitude, 4, stride=NLAT), :]
            out_ref[to, part] = rows.astype(bf16)


def circle(quarters_per_turn, numerator, inverse):
    turns = jnp.floor(numerator * inverse + 0.5)
    v = (numerator - turns * quarters_per_turn) * inverse
    z = v * v
    h = math.pi / 2
    sine = v * (h + z * (-(h**3) / 6 + z * (h**5 / 120 + z * (-(h**7) / 5040))))
    cosine = 1.0 + z * (-(h**2) / 2 + z * (h**4 / 24 + z * (-(h**6) / 720 + z * (h**8 / 40320))))
    halves = jnp.floor(turns * 0.5)
    odd_turn = turns - 2.0 * halves
    flip = 1.0 - 2.0 * is_odd(halves)
    swap = odd_turn > 0.5
    out_cos = jnp.where(swap, sine, cosine) * (flip * (1.0 - 2.0 * odd_turn))
    out_sin = jnp.where(swap, cosine, sine) * flip
    return out_cos, -out_sin


def my_points(me_ref, lat_owner, lat_points):
    latitude = jnp.int32(0)
    for index in range(NLAT):
        latitude = jnp.where(lat_owner[index] == me_ref[0], index % NORTH, latitude)
    return lat_points[latitude]


TILES = QUARTER // LANE
KEPT = 4
STEP = 32


def basis_kernel(
    me_ref, owner_hbm, lat_owner_hbm, lat_points_hbm, after_hbm, near, far_hbm, scale,
    owner, lat_owner, lat_points, waves, far, small, large,
):
    del after_hbm
    copies = [
        pltpu.make_async_copy(owner_hbm, owner, small.at[0]),
        pltpu.make_async_copy(lat_owner_hbm, lat_owner, small.at[1]),
        pltpu.make_async_copy(lat_points_hbm, lat_points, small.at[2]),
    ]
    for copy in copies:
        copy.start()
    for copy in copies:
        copy.wait()
    points = my_points(me_ref, lat_owner, lat_points)
    pair = slot_pairs(jnp.concatenate(owner_rows(owner), axis=1))
    even = jnp.where(is_odd(pair) > 0, TRUNC - pair, pair)
    for index, wave in enumerate((even, TRUNC - even)):
        weight = jnp.where(wave == 0, 1.0, 2.0) * jnp.where(2.0 * wave < points.astype(f32), 1.0, 0.0)
        sign = 1.0 - 2.0 * is_odd(jnp.floor(wave * 0.5))
        scale[2 * index : 2 * index + 1, :] = weight
        scale[2 * index + 1 : 2 * index + 2, :] = weight * sign
        waves[index * PAIRS : (index + 1) * PAIRS, :] = jnp.broadcast_to(to_column(wave), (PAIRS, LANE))
    scale[4:8, :] = jnp.zeros((4, PAIRS), f32)
    quarter = jnp.full((1, LANE), (points // 4).astype(f32))
    inverse = 1.0 / quarter
    column = iota((STEP, LANE), 1).astype(f32)
    outs = []
    for index in range(2):

        def rows_of(block, carry):
            first = pl.multiple_of(block * STEP, STEP)
            wave = waves[pl.ds(index * PAIRS + first, STEP), :]
            cosine, sine = circle(quarter, wave * column, inverse)
            turn_cos, turn_sin = circle(quarter, wave * float(LANE), inverse)
            for tile in range(TILES):
                basis, at = (near, tile) if tile < KEPT else (far, tile - KEPT)
                basis[at, index, pl.ds(first, STEP), :] = cosine.astype(bf16)
                basis[at, index, pl.ds(PAIRS + first, STEP), :] = sine.astype(bf16)
                cosine, sine = cosine * turn_cos - sine * turn_sin, sine * turn_cos + cosine * turn_sin
            return carry

        lax.fori_loop(0, PAIRS // STEP, rows_of, 0)
        for tile in range(TILES - KEPT):
            at = large.at[index * (TILES - KEPT) + tile]
            outs.append(pltpu.make_async_copy(far.at[tile, index], far_hbm.at[tile, index], at))
            outs[-1].start()
    for copy in outs:
        copy.wait()


def fourier_kernel(
    me_ref, lat_owner_hbm, lat_points_hbm, received_ref, scale, near, far_hbm, out_ref,
    lat_owner, lat_points, far, wide, narrow, left, quarters, grid, small, large,
):
    copies = [
        pltpu.make_async_copy(lat_owner_hbm, lat_owner, small.at[0]),
        pltpu.make_async_copy(lat_points_hbm, lat_points, small.at[1]),
    ]
    pieces = [pltpu.make_async_copy(far_hbm.at[tile], far.at[tile], large.at[tile]) for tile in range(TILES - KEPT)]
    for copy in copies + pieces:
        copy.start()
    grid[:, QUARTER:] = jnp.zeros((LEVELS, NLON_PAD - QUARTER), f32)
    for source in range(N_WAVE):
        for part in range(SLOTS // 4):
            wide[pl.ds(source * 24 + 4 * part, 4), :] = received_ref[source, part].astype(f32)
    for slot in range(SLOTS):
        narrow[slot * N_WAVE : (slot + 1) * N_WAVE, :] = wide[pl.ds(slot, N_WAVE, stride=24), :].astype(bf16)
    for copy in copies:
        copy.wait()
    quarter = my_points(me_ref, lat_owner, lat_points) // 4
    out_row, in_col = iota((COLS, COLS), 0), iota((COLS, COLS), 1)
    turn = jnp.where(in_col == 2 * (out_row % LEVELS) + out_row // LEVELS, 1.0, 0.0).astype(bf16)
    for index in range(2):
        turned = lax.dot_general(
            turn,
            narrow[index * PAIRS : (index + 1) * PAIRS, :],
            (((1,), (1,)), ((), ())),
            preferred_element_type=f32,
        )
        weighted = turned * scale[2 * index : 2 * index + 1, :]
        signed = turned * scale[2 * index + 1 : 2 * index + 2, :]
        left[index, :LEVELS, :PAIRS] = weighted[:LEVELS].astype(bf16)
        left[index, :LEVELS, PAIRS:] = weighted[LEVELS:].astype(bf16)
        if index == 0:
            left[index, LEVELS:, :PAIRS] = signed[:LEVELS].astype(bf16)
            left[index, LEVELS:, PAIRS:] = signed[LEVELS:].astype(bf16)
        else:
            left[index, LEVELS:, :PAIRS] = signed[LEVELS:].astype(bf16)
            left[index, LEVELS:, PAIRS:] = -signed[:LEVELS].astype(bf16)
    for first in range(0, QUARTER, 256):
        at = slice(first, min(first + 256, QUARTER))
        tiles = range(first // LANE, at.stop // LANE)
        if tiles.start == KEPT:
            for piece in pieces:
                piece.wait()
        even, odd = [
            jnp.dot(
                left[index],
                jnp.concatenate(
                    [near[tile, index] if tile < KEPT else far[tile - KEPT, index] for tile in tiles], axis=1
                ),
                preferred_element_type=f32,
            )
            for index in range(2)
        ]
        valid = iota((1, even.shape[1]), 1) + first < quarter
        even = jnp.where(valid, even, 0.0)
        odd = jnp.where(valid, odd, 0.0)
        grid[:, at] = even[:LEVELS] + odd[:LEVELS]
        quarters[0, :, at] = even[LEVELS:] - odd[LEVELS:]
        quarters[1, :, at] = even[:LEVELS] - odd[:LEVELS]
        quarters[2, :, at] = even[LEVELS:] + odd[LEVELS:]
    lane = iota((LEVELS, LANE), 1)
    for index in range(3):
        offset = (index + 1) * quarter
        base = pl.multiple_of(offset // LANE * LANE, LANE)
        shift = offset - base
        before = jnp.zeros((LEVELS, LANE), f32)
        for tile in range(QUARTER // LANE + 1):
            if tile < QUARTER // LANE:
                now = pltpu.roll(quarters[index, :, tile * LANE : (tile + 1) * LANE], shift, 1)
            else:
                now = jnp.zeros((LEVELS, LANE), f32)
            at = pl.ds(base + tile * LANE, LANE)
            grid[:, at] = grid[:, at] + jnp.where(lane < shift, before, now)
            before = now
    out_ref[0] = grid[...].astype(bf16)


def params(mib):
    return pltpu.CompilerParams(vmem_limit_bytes=mib * 1024 * 1024)


def per_device(spectral, table, wave_owner, lat_owner, lat_points):
    me = lax.axis_index("wave").astype(jnp.int32).reshape(1)
    waves = wave_owner.shape[0]
    tables = lax.all_gather(table, "lev", axis=0, tiled=False)
    spectral, wave_owner, lat_owner, lat_points = [
        pltpu.with_memory_space_constraint(array, pltpu.HBM)
        for array in (spectral, wave_owner, lat_owner, lat_points)
    ]
    owner_scratch = pltpu.VMEM((waves,), jnp.int32)
    lat_owner_scratch = pltpu.SMEM((NLAT,), jnp.int32)
    lat_points_scratch = pltpu.SMEM((NORTH,), jnp.int32)
    dma = pltpu.SemaphoreType.DMA
    four = pl.pallas_call(
        legendre_kernel,
        out_shape=jax.ShapeDtypeStruct((N_WAVE, SLOTS // 4, 4, COLS), bf16),
        in_specs=[SMEM, HBM, HBM, VMEM, HBM],
        out_specs=VMEM,
        scratch_shapes=[
            owner_scratch,
            lat_owner_scratch,
            pltpu.VMEM((NORTH, ROWS_PAD), f32),
            pltpu.VMEM((ROWS_DEV, COLS), bf16),
            pltpu.VMEM((SLOTS * NLAT, COLS), f32),
            dma((2,)),
            dma((PAIRS_DEV,)),
        ],
        compiler_params=params(24),
        name="legendre",
    )(me, wave_owner, lat_owner, tables, spectral)
    received = lax.all_to_all(four, "wave", split_axis=0, concat_axis=0, tiled=True)
    near_shape = (KEPT, 2, 2 * PAIRS, LANE)
    far_shape = (TILES - KEPT, 2, 2 * PAIRS, LANE)
    near, far, scale = pl.pallas_call(
        basis_kernel,
        out_shape=(pltpu.VMEM(near_shape, bf16), pltpu.HBM(far_shape, bf16), pltpu.VMEM((8, PAIRS), f32)),
        in_specs=[SMEM, HBM, HBM, HBM, HBM],
        out_specs=(VMEM, HBM, VMEM),
        scratch_shapes=[
            owner_scratch,
            lat_owner_scratch,
            lat_points_scratch,
            pltpu.VMEM((2 * PAIRS, LANE), f32),
            pltpu.VMEM(far_shape, bf16),
            dma((3,)),
            dma((2 * (TILES - KEPT),)),
        ],
        compiler_params=params(16),
        name="basis",
    )(me, wave_owner, lat_owner, lat_points, pltpu.with_memory_space_constraint(four, pltpu.HBM))
    return pl.pallas_call(
        fourier_kernel,
        out_shape=jax.ShapeDtypeStruct((1, LEVELS, NLON_PAD), bf16),
        in_specs=[SMEM, HBM, HBM, VMEM, VMEM, VMEM, HBM],
        out_specs=VMEM,
        scratch_shapes=[
            lat_owner_scratch,
            lat_points_scratch,
            pltpu.VMEM(far_shape, bf16),
            pltpu.VMEM((N_WAVE * 24, COLS), f32),
            pltpu.VMEM((SLOTS * N_WAVE, COLS), bf16),
            pltpu.VMEM((2, COLS, 2 * PAIRS), bf16),
            pltpu.VMEM((3, LEVELS, QUARTER), f32),
            pltpu.VMEM((LEVELS, NLON_PAD), f32),
            dma((2,)),
            dma((TILES - KEPT,)),
        ],
        compiler_params=params(24),
        name="fourier",
    )(
        me,
        lat_owner,
        lat_points,
        received,
        pltpu.with_memory_space_constraint(scale, pltpu.VMEM),
        pltpu.with_memory_space_constraint(near, pltpu.VMEM),
        pltpu.with_memory_space_constraint(far, pltpu.HBM),
    )


def solution(mesh):
    in_specs = (P("wave", "lev"), P("lev", "wave"), P(), P(), P())
    out_specs = P("wave", "lev", None)
    return jax.shard_map(
        per_device, mesh=mesh, in_specs=in_specs, out_specs=out_specs, check_vma=False
    )
```

time: 64.5 us -> 55.8 us (0.87)
  local copies, waits for them, and re-layouts: 13.8 us -> 0 us
  waiting for transfers between devices: 6.26 us -> 9.26 us
  Pallas kernels: 13.5 us -> 15.9 us
    unnamed x20 -> x0, local copies, waits for them, and re-layouts: 12.6 us -> none
    all_to_all x1, waiting for transfers between devices: 6.26 us -> 9.26 us  [per_device(): lax.all_to_all(four, 'wave', split_axis=0, concat_axis=0, tiled=True)]
    pallas_call x1, Pallas kernels: 3.17 us -> 4.44 us  [per_device(): pl.pallas_call(legendre_kernel, out_shape=jax.ShapeDtypeStruct((N_WAVE, S...]
    pallas_call x1, Pallas kernels: 3.35 us -> 4.44 us  [per_device(): pl.pallas_call(fourier_kernel, out_shape=jax.ShapeDtypeStruct((1, LEVELS,...]
    slice x1 -> x0, local copies, waits for them, and re-layouts: 0.69 us -> none  [per_device(): owner_row = wave_owner[:PAIRS].reshape(1, PAIRS)]
    pallas_call x2 -> x1, Pallas kernels: 7.01 us -> 6.97 us  [per_device(): pl.pallas_call(basis_kernel, out_shape=(pltpu.VMEM(near_shape, bf16), plt...]
  transfers between devices with their start and end apart: 1 -> 1, of which waited for: 1 -> 1; matrix products, arithmetic and copies ran while one was open for 0% -> 0% of each run, Pallas kernels for 8% -> 13%
where the time goes in v2:
time: 55.8 us; the launch traced here: 55.5 us
  blocking collectives  17 us (30%)
  Pallas kernels  15.9 us (28%)
  starting transfers between devices  13.4 us (24%)
  waiting for transfers between devices  9.26 us (17%)
    all_gather x1, blocking collectives, per_device(): tables = lax.all_gather(table, 'lev', axis=0, tiled=False)  17 us
    all_to_all x1, starting transfers between devices, per_device(): lax.all_to_all(four, 'wave', split_axis=0, concat_axis=0, tiled=True)  13.4 us
    all_to_all x1, waiting for transfers between devices, per_device(): lax.all_to_all(four, 'wave', split_axis=0, concat_axis=0, tiled=True)  9.26 us
    pallas_call x1, Pallas kernels, per_device(): pl.pallas_call(basis_kernel, out_shape=(pltpu.VMEM(near_shape, bf16), plt...  6.97 us
    pallas_call x1, Pallas kernels, per_device(): pl.pallas_call(fourier_kernel, out_shape=jax.ShapeDtypeStruct((1, LEVELS,...  4.44 us
    pallas_call x1, Pallas kernels, per_device(): pl.pallas_call(legendre_kernel, out_shape=jax.ShapeDtypeStruct((N_WAVE, S...  4.44 us
  transfers between devices with their start and end apart: 1, of which 1 were waited for; matrix products, arithmetic and copies ran while one was open for 0% of the time, Pallas kernels for 13%

profile of v2, /device:TPU:2, one launch (start us, length us, event | category | flops | bytes accessed | tf_op | source)
XLA Modules:
  0.0 55.5 jit_solution(9402262285512727353)
XLA Ops:
  0.0 17.0 %all-gather.1.table_ref = bf16[8,4,12820]{2,1,0:T(4,128)(2,1)S(1)} all-gather(bf16[1,4,12820]{2,1,0:T(4,128)(2,1)} %bitcast.2), channel_id=2, replica_groups=mesh['wave'=64,'lev'=8] {'lev'}, dimensions={0}, use_global_device_ids=true | all-gather | bytes 923040 | tf_op jit(solution)/shard_map/all_gather | solution.py:313
  17.0 4.4 %legendre.1.after_hbm = bf16[64,5,4,128]{3,2,1,0:T(4,128)(2,1)} custom-call(s32[1]{0:T(128)} %bitcast.me_ref, s32[1280]{0:T(1024)} %owner_hbm.3, s32[64]{0:T(128)} %lat_owner_hbm.5, bf16[8,4,12820]{2,1,0:T(4,128)(2,1)S(1)} %all-gather.1.table_ref, bf16[12820,128]{1,0:T(8,128)(2,1)} %spectral_hbm.1), custom_call_target="tpu_custom_call" | custom-call | tf_op jit(solution)/shard_map/legendre/pallas_call | solution.py:322
  21.5 13.4 %all-to-all-start = ((bf16[64,5,4,128]{3,2,1,0:T(4,128)(2,1)}), bf16[64,5,4,128]{3,2,1,0:T(4,128)(2,1)S(1)}, u32[]{:S(2)}, u32[]{:S(2)}) async-start(bf16[64,5,4,128]{3,2,1,0:T(4,128)(2,1)} %legendre.1.after_hbm), calls=%async_computation | async-start | bytes 655360 | tf_op jit(solution)/shard_map/all_to_all | solution.py:339
  34.9 7.0 %basis.1 = (bf16[4,2,1280,128]{3,2,1,0:T(8,128)(2,1)S(1)}, bf16[7,2,1280,128]{3,2,1,0:T(8,128)(2,1)}, f32[8,640]{1,0:T(8,128)S(1)}) custom-call(s32[1]{0:T(128)} %bitcast.me_ref, s32[1280]{0:T(1024)} %owner_hbm.3, s32[64]{0:T(128)} %lat_owner_hbm.5, s32[32]{0:T(128)} %lat_points_hbm.3, bf16[64,5,4,128]{3,2,1,0:T(4,128)(2,1)} %legendre.1.after_hbm), custom_call_target="tpu_custom_call" | custom-call | tf_op jit(solution)/shard_map/basis/pallas_call | solution.py:342
  41.8 9.3 %all-to-all-done.received_ref = bf16[64,5,4,128]{3,2,1,0:T(4,128)(2,1)S(1)} async-done(((bf16[64,5,4,128]{3,2,1,0:T(4,128)(2,1)}), bf16[64,5,4,128]{3,2,1,0:T(4,128)(2,1)S(1)}, u32[]{:S(2)}, u32[]{:S(2)}) %all-to-all-start) | async-done | bytes 327712 | tf_op jit(solution)/shard_map/all_to_all | solution.py:339
  51.1 4.4 %fourier.1 = bf16[1,64,5376]{2,1,0:T(8,128)(2,1)} custom-call(s32[1]{0:T(128)} %bitcast.me_ref, s32[64]{0:T(128)} %lat_owner_hbm.5, s32[32]{0:T(128)} %lat_points_hbm.3, bf16[64,5,4,128]{3,2,1,0:T(4,128)(2,1)S(1)} %all-to-all-done.received_ref, f32[8,640]{1,0:T(8,128)S(1)} %get-tuple-element.8.scale, bf16[4,2,1280,128]{3,2,1,0:T(8,128)(2,1)S(1)} %get-tuple-element.9.near, ...), custom_call_target="tpu_custom_call" | custom-call | tf_op jit(solution)/shard_map/fourier/pallas_call | solution.py:359
Async XLA Ops:
  21.5 29.6 %all-to-all-start = ((bf16[64,5,4,128]{3,2,1,0:T(4,128)(2,1)}), bf16[64,5,4,128]{3,2,1,0:T(4,128)(2,1)S(1)}, u32[]{:S(2)}, u32[]{:S(2)}) async-start(bf16[64,5,4,128]{3,2,1,0:T(4,128)(2,1)} %legendre.1.after_hbm), calls=%async_computation | async-start | bytes 655360 | tf_op jit(solution)/shard_map/all_to_all | solution.py:339

commit v3 on v2

--- a/solution.py
+++ b/solution.py
@@ -19,7 +19,7 @@
 LEVELS = 64
 COLS = 128
 SLOTS = 20
-QUARTER = 1408
+EIGHTH = 768
 NLON_PAD = 5376
 LANE = 128
 
@@ -168,7 +168,9 @@
     return lat_points[latitude]
 
 
-TILES = QUARTER // LANE
+TILES = EIGHTH // LANE
+MARGIN = TILES + 1
+GROUP = 32
 KEPT = 4
 STEP = 32
 
@@ -225,8 +227,8 @@
 
 
 def fourier_kernel(
-    me_ref, lat_owner_hbm, lat_points_hbm, received_ref, scale, near, far_hbm, out_ref,
-    lat_owner, lat_points, far, wide, narrow, left, quarters, grid, small, large,
+    me_ref, lat_owner_hbm, lat_points_hbm, received_ref, scale, near, far_hbm, out_hbm,
+    lat_owner, lat_points, far, wide, narrow, left, ahead, back, grid, rounded, small, large,
 ):
     copies = [
         pltpu.make_async_copy(lat_owner_hbm, lat_owner, small.at[0]),
@@ -235,15 +237,12 @@
     pieces = [pltpu.make_async_copy(far_hbm.at[tile], far.at[tile], large.at[tile]) for tile in range(TILES - KEPT)]
     for copy in copies + pieces:
         copy.start()
-    grid[:, QUARTER:] = jnp.zeros((LEVELS, NLON_PAD - QUARTER), f32)
+    grid[...] = jnp.zeros(grid.shape, f32)
     for source in range(N_WAVE):
         for part in range(SLOTS // 4):
             wide[pl.ds(source * 24 + 4 * part, 4), :] = received_ref[source, part].astype(f32)
     for slot in range(SLOTS):
         narrow[slot * N_WAVE : (slot + 1) * N_WAVE, :] = wide[pl.ds(slot, N_WAVE, stride=24), :].astype(bf16)
-    for copy in copies:
-        copy.wait()
-    quarter = my_points(me_ref, lat_owner, lat_points) // 4
     out_row, in_col = iota((COLS, COLS), 0), iota((COLS, COLS), 1)
     turn = jnp.where(in_col == 2 * (out_row % LEVELS) + out_row // LEVELS, 1.0, 0.0).astype(bf16)
     for index in range(2):
@@ -255,52 +254,85 @@
         )
         weighted = turned * scale[2 * index : 2 * index + 1, :]
         signed = turned * scale[2 * index + 1 : 2 * index + 2, :]
-        left[index, :LEVELS, :PAIRS] = weighted[:LEVELS].astype(bf16)
-        left[index, :LEVELS, PAIRS:] = weighted[LEVELS:].astype(bf16)
+        left[index, 0, :LEVELS] = weighted[:LEVELS].astype(bf16)
+        left[index, 1, :LEVELS] = weighted[LEVELS:].astype(bf16)
         if index == 0:
-            left[index, LEVELS:, :PAIRS] = signed[:LEVELS].astype(bf16)
-            left[index, LEVELS:, PAIRS:] = signed[LEVELS:].astype(bf16)
+            left[index, 0, LEVELS:] = signed[:LEVELS].astype(bf16)
+            left[index, 1, LEVELS:] = signed[LEVELS:].astype(bf16)
         else:
-            left[index, LEVELS:, :PAIRS] = signed[LEVELS:].astype(bf16)
-            left[index, LEVELS:, PAIRS:] = -signed[:LEVELS].astype(bf16)
-    for first in range(0, QUARTER, 256):
-        at = slice(first, min(first + 256, QUARTER))
-        tiles = range(first // LANE, at.stop // LANE)
+            left[index, 0, LEVELS:] = signed[LEVELS:].astype(bf16)
+            left[index, 1, LEVELS:] = -signed[:LEVELS].astype(bf16)
+    for copy in copies:
+        copy.wait()
+    quarter = my_points(me_ref, lat_owner, lat_points) // 4
+    half = quarter // 2
+    for first in range(0, EIGHTH, 2 * LANE):
+        at = slice(first, first + 2 * LANE)
+        tiles = range(first // LANE, first // LANE + 2)
         if tiles.start == KEPT:
             for piece in pieces:
                 piece.wait()
-        even, odd = [
-            jnp.dot(
-                left[index],
-                jnp.concatenate(
-                    [near[tile, index] if tile < KEPT else far[tile - KEPT, index] for tile in tiles], axis=1
-                ),
-                preferred_element_type=f32,
+        sums = []
+        for index in range(2):
+            right = jnp.concatenate(
+                [near[tile, index] if tile < KEPT else far[tile - KEPT, index] for tile in tiles], axis=1
             )
-            for index in range(2)
-        ]
-        valid = iota((1, even.shape[1]), 1) + first < quarter
-        even = jnp.where(valid, even, 0.0)
-        odd = jnp.where(valid, odd, 0.0)
-        grid[:, at] = even[:LEVELS] + odd[:LEVELS]
-        quarters[0, :, at] = even[LEVELS:] - odd[LEVELS:]
-        quarters[1, :, at] = even[:LEVELS] - odd[:LEVELS]
-        quarters[2, :, at] = even[LEVELS:] + odd[LEVELS:]
-    lane = iota((LEVELS, LANE), 1)
-    for index in range(3):
-        offset = (index + 1) * quarter
-        base = pl.multiple_of(offset // LANE * LANE, LANE)
-        shift = offset - base
-        before = jnp.zeros((LEVELS, LANE), f32)
-        for tile in range(QUARTER // LANE + 1):
-            if tile < QUARTER // LANE:
-                now = pltpu.roll(quarters[index, :, tile * LANE : (tile + 1) * LANE], shift, 1)
-            else:
-                now = jnp.zeros((LEVELS, LANE), f32)
-            at = pl.ds(base + tile * LANE, LANE)
-            grid[:, at] = grid[:, at] + jnp.where(lane < shift, before, now)
-            before = now
-    out_ref[0] = grid[...].astype(bf16)
+            sums.append(jnp.dot(left[index, 0], right[:PAIRS], preferred_element_type=f32))
+            sums.append(jnp.dot(left[index, 1], right[PAIRS:], preferred_element_type=f32))
+        even_cos, even_sin, odd_cos, odd_sin = sums
+        even, odd = even_cos + even_sin, odd_cos + odd_sin
+        ahead[0, :, at] = even[:LEVELS] + odd[:LEVELS]
+        ahead[1, :, at] = even[LEVELS:] - odd[LEVELS:]
+        ahead[2, :, at] = even[:LEVELS] - odd[:LEVELS]
+        ahead[3, :, at] = even[LEVELS:] + odd[LEVELS:]
+        even, odd = even_cos - even_sin, odd_cos - odd_sin
+        back[0, :, at] = even[LEVELS:] - odd[LEVELS:]
+        back[1, :, at] = even[:LEVELS] - odd[:LEVELS]
+        back[2, :, at] = even[LEVELS:] + odd[LEVELS:]
+        back[3, :, at] = even[:LEVELS] + odd[:LEVELS]
+    lane = iota((GROUP, LANE), 1)
+    zero = jnp.zeros((GROUP, LANE), f32)
+    outs = []
+    for group in range(LEVELS // GROUP):
+        rows = slice(group * GROUP, (group + 1) * GROUP)
+
+        def put(tile, value, first, last):
+            at = pl.ds(pl.multiple_of((tile + MARGIN) * LANE, LANE), LANE)
+            point = lane + tile * LANE
+            pltpu.store(grid.at[rows, at], value, mask=(point >= first) & (point <= last))
+
+        for index in range(4):
+            offset = index * quarter
+            shift = offset % LANE
+            before = zero
+            for tile in range(TILES + (1 if index else 0)):
+                now = zero
+                if tile < TILES:
+                    now = ahead[index, rows, tile * LANE : (tile + 1) * LANE]
+                    if index:
+                        now = pltpu.roll(now, shift, 1)
+                value = jnp.where(lane < shift, before, now) if index else now
+                put(offset // LANE + tile, value, offset, offset + half)
+                before = now
+            offset = (index + 1) * quarter
+            shift = offset % LANE
+            order = lax.rem(shift - lane + LANE, LANE)
+            before = zero
+            for tile in range(TILES + 1):
+                now = zero
+                if tile < TILES:
+                    now = jnp.take_along_axis(
+                        back[index, rows, tile * LANE : (tile + 1) * LANE], order, axis=1, mode="promise_in_bounds"
+                    )
+                value = jnp.where(lane <= shift, now, before)
+                put(offset // LANE - tile, value, index * quarter + half + 1, offset - 1)
+                before = now
+        rounded[rows, :] = grid[rows, MARGIN * LANE :].astype(bf16)
+        at = pl.ds(group * GROUP, GROUP)
+        outs.append(pltpu.make_async_copy(rounded.at[at], out_hbm.at[0, at], small.at[2 + group]))
+        outs[-1].start()
+    for copy in outs:
+        copy.wait()
 
 
 def params(mib):
@@ -358,19 +390,21 @@
     )(me, wave_owner, lat_owner, lat_points, pltpu.with_memory_space_constraint(four, pltpu.HBM))
     return pl.pallas_call(
         fourier_kernel,
-        out_shape=jax.ShapeDtypeStruct((1, LEVELS, NLON_PAD), bf16),
+        out_shape=pltpu.HBM((1, LEVELS, NLON_PAD), bf16),
         in_specs=[SMEM, HBM, HBM, VMEM, VMEM, VMEM, HBM],
-        out_specs=VMEM,
+        out_specs=HBM,
         scratch_shapes=[
             lat_owner_scratch,
             lat_points_scratch,
             pltpu.VMEM(far_shape, bf16),
             pltpu.VMEM((N_WAVE * 24, COLS), f32),
             pltpu.VMEM((SLOTS * N_WAVE, COLS), bf16),
-            pltpu.VMEM((2, COLS, 2 * PAIRS), bf16),
-            pltpu.VMEM((3, LEVELS, QUARTER), f32),
-            pltpu.VMEM((LEVELS, NLON_PAD), f32),
-            dma((2,)),
+            pltpu.VMEM((2, 2, COLS, PAIRS), bf16),
+            pltpu.VMEM((4, LEVELS, EIGHTH), f32),
+            pltpu.VMEM((4, LEVELS, EIGHTH), f32),
+            pltpu.VMEM((LEVELS, MARGIN * LANE + NLON_PAD), f32),
+            pltpu.VMEM((LEVELS, NLON_PAD), bf16),
+            dma((2 + LEVELS // GROUP,)),
             dma((TILES - KEPT,)),
         ],
         compiler_params=params(24),

time: 55.8 us -> 54.3 us (0.973)
  Pallas kernels: 15.9 us -> 13 us
  waiting for transfers between devices: 9.26 us -> 10.6 us
    pallas_call x1, Pallas kernels: 4.44 us -> 3 us  [per_device(): pl.pallas_call(fourier_kernel, out_shape=pltpu.HBM((1, LEVELS, NLON_PAD),...]
    all_to_all x1, waiting for transfers between devices: 9.26 us -> 10.6 us  [per_device(): lax.all_to_all(four, 'wave', split_axis=0, concat_axis=0, tiled=True)]
    pallas_call x1, Pallas kernels: 6.97 us -> 5.6 us  [per_device(): pl.pallas_call(basis_kernel, out_shape=(pltpu.VMEM(near_shape, bf16), plt...]
  transfers between devices with their start and end apart: 1 -> 1, of which waited for: 1 -> 1; matrix products, arithmetic and copies ran while one was open for 0% -> 0% of each run, Pallas kernels for 13% -> 10%
where the time goes in v3:
time: 54.3 us; the launch traced here: 54.1 us
  blocking collectives  17 us (31%)
  starting transfers between devices  13.4 us (25%)
  Pallas kernels  13 us (24%)
  waiting for transfers between devices  10.6 us (20%)
    all_gather x1, blocking collectives, per_device(): tables = lax.all_gather(table, 'lev', axis=0, tiled=False)  17 us
    all_to_all x1, starting transfers between devices, per_device(): lax.all_to_all(four, 'wave', split_axis=0, concat_axis=0, tiled=True)  13.4 us
    all_to_all x1, waiting for transfers between devices, per_device(): lax.all_to_all(four, 'wave', split_axis=0, concat_axis=0, tiled=True)  10.6 us
    pallas_call x1, Pallas kernels, per_device(): pl.pallas_call(basis_kernel, out_shape=(pltpu.VMEM(near_shape, bf16), plt...  5.6 us
    pallas_call x1, Pallas kernels, per_device(): pl.pallas_call(legendre_kernel, out_shape=jax.ShapeDtypeStruct((N_WAVE, S...  4.41 us
    pallas_call x1, Pallas kernels, per_device(): pl.pallas_call(fourier_kernel, out_shape=pltpu.HBM((1, LEVELS, NLON_PAD),...  3 us
  transfers between devices with their start and end apart: 1, of which 1 were waited for; matrix products, arithmetic and copies ran while one was open for 0% of the time, Pallas kernels for 10%

profile of v3, /device:TPU:2, one launch (start us, length us, event | category | flops | bytes accessed | tf_op | source)
XLA Modules:
  0.0 54.1 jit_solution(13241002604937360599)
XLA Ops:
  0.0 17.0 %all-gather.1.table_ref = bf16[8,4,12820]{2,1,0:T(4,128)(2,1)S(1)} all-gather(bf16[1,4,12820]{2,1,0:T(4,128)(2,1)} %bitcast.2), channel_id=2, replica_groups=mesh['wave'=64,'lev'=8] {'lev'}, dimensions={0}, use_global_device_ids=true | all-gather | bytes 923040 | tf_op jit(solution)/shard_map/all_gather | solution.py:345
  17.0 4.4 %legendre.1.after_hbm = bf16[64,5,4,128]{3,2,1,0:T(4,128)(2,1)} custom-call(s32[1]{0:T(128)} %bitcast.me_ref, s32[1280]{0:T(1024)} %owner_hbm.3, s32[64]{0:T(128)} %lat_owner_hbm.5, bf16[8,4,12820]{2,1,0:T(4,128)(2,1)S(1)} %all-gather.1.table_ref, bf16[12820,128]{1,0:T(8,128)(2,1)} %spectral_hbm.1), custom_call_target="tpu_custom_call" | custom-call | tf_op jit(solution)/shard_map/legendre/pallas_call | solution.py:354
  21.5 13.4 %all-to-all-start = ((bf16[64,5,4,128]{3,2,1,0:T(4,128)(2,1)}), bf16[64,5,4,128]{3,2,1,0:T(4,128)(2,1)S(1)}, u32[]{:S(2)}, u32[]{:S(2)}) async-start(bf16[64,5,4,128]{3,2,1,0:T(4,128)(2,1)} %legendre.1.after_hbm), calls=%async_computation | async-start | bytes 655360 | tf_op jit(solution)/shard_map/all_to_all | solution.py:371
  34.8 5.6 %basis.1 = (bf16[4,2,1280,128]{3,2,1,0:T(8,128)(2,1)S(1)}, bf16[2,2,1280,128]{3,2,1,0:T(8,128)(2,1)}, f32[8,640]{1,0:T(8,128)S(1)}) custom-call(s32[1]{0:T(128)} %bitcast.me_ref, s32[1280]{0:T(1024)} %owner_hbm.3, s32[64]{0:T(128)} %lat_owner_hbm.5, s32[32]{0:T(128)} %lat_points_hbm.3, bf16[64,5,4,128]{3,2,1,0:T(4,128)(2,1)} %legendre.1.after_hbm), custom_call_target="tpu_custom_call" | custom-call | tf_op jit(solution)/shard_map/basis/pallas_call | solution.py:374
  40.4 10.6 %all-to-all-done.received_ref = bf16[64,5,4,128]{3,2,1,0:T(4,128)(2,1)S(1)} async-done(((bf16[64,5,4,128]{3,2,1,0:T(4,128)(2,1)}), bf16[64,5,4,128]{3,2,1,0:T(4,128)(2,1)S(1)}, u32[]{:S(2)}, u32[]{:S(2)}) %all-to-all-start) | async-done | bytes 327712 | tf_op jit(solution)/shard_map/all_to_all | solution.py:371
  51.1 3.0 %fourier.1 = bf16[1,64,5376]{2,1,0:T(8,128)(2,1)} custom-call(s32[1]{0:T(128)} %bitcast.me_ref, s32[64]{0:T(128)} %lat_owner_hbm.5, s32[32]{0:T(128)} %lat_points_hbm.3, bf16[64,5,4,128]{3,2,1,0:T(4,128)(2,1)S(1)} %all-to-all-done.received_ref, f32[8,640]{1,0:T(8,128)S(1)} %get-tuple-element.8.scale, bf16[4,2,1280,128]{3,2,1,0:T(8,128)(2,1)S(1)} %get-tuple-element.9.near, ...), custom_call_target="tpu_custom_call" | custom-call | tf_op jit(solution)/shard_map/fourier/pallas_call | solution.py:391
Async XLA Ops:
  21.5 29.6 %all-to-all-start = ((bf16[64,5,4,128]{3,2,1,0:T(4,128)(2,1)}), bf16[64,5,4,128]{3,2,1,0:T(4,128)(2,1)S(1)}, u32[]{:S(2)}, u32[]{:S(2)}) async-start(bf16[64,5,4,128]{3,2,1,0:T(4,128)(2,1)} %legendre.1.after_hbm), calls=%async_computation | async-start | bytes 655360 | tf_op jit(solution)/shard_map/all_to_all | solution.py:371

commit v4 on v3

--- a/solution.py
+++ b/solution.py
@@ -96,6 +96,9 @@
     return min(-(-PAIR_ROWS * (pair + 1) // LANE) * LANE, ROWS_DEV)
 
 
+PIECES = (0, 2, 5)
+
+
 def legendre_kernel(
     me_ref, owner_hbm, lat_owner_hbm, table_ref, spectral_hbm, out_ref, owner, lat_owner, table, spectral, four, small, large
 ):
@@ -103,16 +106,17 @@
         pltpu.make_async_copy(owner_hbm, owner, small.at[0]),
         pltpu.make_async_copy(lat_owner_hbm, lat_owner, small.at[1]),
     ]
-    pieces = []
-    for pair in range(PAIRS_DEV):
+    pieces = {}
+    for index, (pair, end) in enumerate(zip(PIECES, PIECES[1:] + (PAIRS_DEV,))):
         start = last_row(pair - 1) if pair else 0
-        at = pl.ds(start, last_row(pair) - start)
-        pieces.append(pltpu.make_async_copy(spectral_hbm.at[at], spectral.at[at], large.at[pair]))
-    for copy in copies + pieces:
+        at = pl.ds(start, last_row(end - 1) - start)
+        pieces[pair] = pltpu.make_async_copy(spectral_hbm.at[at], spectral.at[at], large.at[index])
+    for copy in copies + list(pieces.values()):
         copy.start()
     for index in range(8):
         table[4 * index : 4 * index + 4, 0:ROWS_DEV] = table_ref[index].astype(f32)
-    copies[0].wait()
+    for copy in copies:
+        copy.wait()
     locals_ = local_pairs(owner_rows(owner), me_ref[0].astype(f32))
     for pair in range(PAIRS_DEV):
         start, stop = first_row(pair), last_row(pair)
@@ -127,22 +131,19 @@
         odd = low + high - even
         odd_sign = 1.0 - 2.0 * is_odd(row)
         even_sign = odd_sign * (1.0 - 2.0 * q_odd)
-        block = table[:, start:stop]
+        block = table[:, start:stop].astype(bf16)
         left = jnp.concatenate(
-            [block * even, block * (even * even_sign), block * odd, block * (odd * odd_sign)], axis=0
-        ).astype(bf16)
-        if pair in (0, 5):
-            for piece in pieces[pair : pair + 5]:
-                piece.wait()
+            [block * mask.astype(bf16) for mask in (even, even * even_sign, odd, odd * odd_sign)], axis=0
+        )
+        if pair in pieces:
+            pieces[pair].wait()
         values = jnp.dot(left, spectral[start:stop, :], preferred_element_type=f32)
-        four[pair * NLAT : (pair + 1) * NLAT, :] = values[:NLAT]
-        four[(PAIRS_DEV + pair) * NLAT : (PAIRS_DEV + pair + 1) * NLAT, :] = values[NLAT:]
-    copies[1].wait()
-    for latitude in range(NLAT):
-        to = lat_owner[latitude]
-        for part in range(SLOTS // 4):
-            rows = four[pl.ds(4 * part * NLAT + latitude, 4, stride=NLAT), :]
-            out_ref[to, part] = rows.astype(bf16)
+        four[2 * pair * NLAT : 2 * (pair + 1) * NLAT, :] = values
+        if pair % 2 == 1:
+            part = pair // 2
+            for latitude in range(NLAT):
+                rows = four[pl.ds(4 * part * NLAT + latitude, 4, stride=NLAT), :]
+                out_ref[lat_owner[latitude], part] = rows.astype(bf16)
 
 
 def circle(quarters_per_turn, numerator, inverse):
@@ -241,8 +242,11 @@
     for source in range(N_WAVE):
         for part in range(SLOTS // 4):
             wide[pl.ds(source * 24 + 4 * part, 4), :] = received_ref[source, part].astype(f32)
-    for slot in range(SLOTS):
-        narrow[slot * N_WAVE : (slot + 1) * N_WAVE, :] = wide[pl.ds(slot, N_WAVE, stride=24), :].astype(bf16)
+    for index in range(2):
+        for pair in range(PAIRS_DEV):
+            slot = index * PAIRS_DEV + pair
+            rows = wide[pl.ds(2 * pair + index, N_WAVE, stride=24), :]
+            narrow[slot * N_WAVE : (slot + 1) * N_WAVE, :] = rows.astype(bf16)
     out_row, in_col = iota((COLS, COLS), 0), iota((COLS, COLS), 1)
     turn = jnp.where(in_col == 2 * (out_row % LEVELS) + out_row // LEVELS, 1.0, 0.0).astype(bf16)
     for index in range(2):
@@ -363,7 +367,7 @@
             pltpu.VMEM((ROWS_DEV, COLS), bf16),
             pltpu.VMEM((SLOTS * NLAT, COLS), f32),
             dma((2,)),
-            dma((PAIRS_DEV,)),
+            dma((len(PIECES),)),
         ],
         compiler_params=params(24),
         name="legendre",

time: 54.3 us -> 53.6 us (0.987)
  Pallas kernels: 13 us -> 12.4 us
    pallas_call x1, Pallas kernels: 4.41 us -> 3.76 us  [per_device(): pl.pallas_call(legendre_kernel, out_shape=jax.ShapeDtypeStruct((N_WAVE, S...]
where the time goes in v4:
time: 53.6 us; the launch traced here: 53.4 us
  blocking collectives  17 us (32%)
  starting transfers between devices  13.4 us (25%)
  Pallas kernels  12.4 us (23%)
  waiting for transfers between devices  10.6 us (20%)
    all_gather x1, blocking collectives, per_device(): tables = lax.all_gather(table, 'lev', axis=0, tiled=False)  17 us
    all_to_all x1, starting transfers between devices, per_device(): lax.all_to_all(four, 'wave', split_axis=0, concat_axis=0, tiled=True)  13.4 us
    all_to_all x1, waiting for transfers between devices, per_device(): lax.all_to_all(four, 'wave', split_axis=0, concat_axis=0, tiled=True)  10.6 us
    pallas_call x1, Pallas kernels, per_device(): pl.pallas_call(basis_kernel, out_shape=(pltpu.VMEM(near_shape, bf16), plt...  5.6 us
    pallas_call x1, Pallas kernels, per_device(): pl.pallas_call(legendre_kernel, out_shape=jax.ShapeDtypeStruct((N_WAVE, S...  3.76 us
    pallas_call x1, Pallas kernels, per_device(): pl.pallas_call(fourier_kernel, out_shape=pltpu.HBM((1, LEVELS, NLON_PAD),...  3 us
  transfers between devices with their start and end apart: 1, of which 1 were waited for; matrix products, arithmetic and copies ran while one was open for 0% of the time, Pallas kernels for 10%

profile of v4, /device:TPU:2, one launch (start us, length us, event | category | flops | bytes accessed | tf_op | source)
XLA Modules:
  0.0 53.4 jit_solution(13012093165000800075)
XLA Ops:
  0.0 17.0 %all-gather.1.table_ref = bf16[8,4,12820]{2,1,0:T(4,128)(2,1)S(1)} all-gather(bf16[1,4,12820]{2,1,0:T(4,128)(2,1)} %bitcast.2), channel_id=2, replica_groups=mesh['wave'=64,'lev'=8] {'lev'}, dimensions={0}, use_global_device_ids=true | all-gather | bytes 923040 | tf_op jit(solution)/shard_map/all_gather | solution.py:349
  17.0 3.8 %legendre.1.after_hbm = bf16[64,5,4,128]{3,2,1,0:T(4,128)(2,1)} custom-call(s32[1]{0:T(128)} %bitcast.me_ref, s32[1280]{0:T(1024)} %owner_hbm.3, s32[64]{0:T(128)} %lat_owner_hbm.5, bf16[8,4,12820]{2,1,0:T(4,128)(2,1)S(1)} %all-gather.1.table_ref, bf16[12820,128]{1,0:T(8,128)(2,1)} %spectral_hbm.1), custom_call_target="tpu_custom_call" | custom-call | tf_op jit(solution)/shard_map/legendre/pallas_call | solution.py:358
  20.8 13.4 %all-to-all-start = ((bf16[64,5,4,128]{3,2,1,0:T(4,128)(2,1)}), bf16[64,5,4,128]{3,2,1,0:T(4,128)(2,1)S(1)}, u32[]{:S(2)}, u32[]{:S(2)}) async-start(bf16[64,5,4,128]{3,2,1,0:T(4,128)(2,1)} %legendre.1.after_hbm), calls=%async_computation | async-start | bytes 655360 | tf_op jit(solution)/shard_map/all_to_all | solution.py:375
  34.2 5.6 %basis.1 = (bf16[4,2,1280,128]{3,2,1,0:T(8,128)(2,1)S(1)}, bf16[2,2,1280,128]{3,2,1,0:T(8,128)(2,1)}, f32[8,640]{1,0:T(8,128)S(1)}) custom-call(s32[1]{0:T(128)} %bitcast.me_ref, s32[1280]{0:T(1024)} %owner_hbm.3, s32[64]{0:T(128)} %lat_owner_hbm.5, s32[32]{0:T(128)} %lat_points_hbm.3, bf16[64,5,4,128]{3,2,1,0:T(4,128)(2,1)} %legendre.1.after_hbm), custom_call_target="tpu_custom_call" | custom-call | tf_op jit(solution)/shard_map/basis/pallas_call | solution.py:378
  39.8 10.6 %all-to-all-done.received_ref = bf16[64,5,4,128]{3,2,1,0:T(4,128)(2,1)S(1)} async-done(((bf16[64,5,4,128]{3,2,1,0:T(4,128)(2,1)}), bf16[64,5,4,128]{3,2,1,0:T(4,128)(2,1)S(1)}, u32[]{:S(2)}, u32[]{:S(2)}) %all-to-all-start) | async-done | bytes 327712 | tf_op jit(solution)/shard_map/all_to_all | solution.py:375
  50.4 3.0 %fourier.1 = bf16[1,64,5376]{2,1,0:T(8,128)(2,1)} custom-call(s32[1]{0:T(128)} %bitcast.me_ref, s32[64]{0:T(128)} %lat_owner_hbm.5, s32[32]{0:T(128)} %lat_points_hbm.3, bf16[64,5,4,128]{3,2,1,0:T(4,128)(2,1)S(1)} %all-to-all-done.received_ref, f32[8,640]{1,0:T(8,128)S(1)} %get-tuple-element.8.scale, bf16[4,2,1280,128]{3,2,1,0:T(8,128)(2,1)S(1)} %get-tuple-element.9.near, ...), custom_call_target="tpu_custom_call" | custom-call | tf_op jit(solution)/shard_map/fourier/pallas_call | solution.py:395
Async XLA Ops:
  20.8 29.6 %all-to-all-start = ((bf16[64,5,4,128]{3,2,1,0:T(4,128)(2,1)}), bf16[64,5,4,128]{3,2,1,0:T(4,128)(2,1)S(1)}, u32[]{:S(2)}, u32[]{:S(2)}) async-start(bf16[64,5,4,128]{3,2,1,0:T(4,128)(2,1)} %legendre.1.after_hbm), calls=%async_computation | async-start | bytes 655360 | tf_op jit(solution)/shard_map/all_to_all | solution.py:375

commit v5 on v4

--- a/solution.py
+++ b/solution.py
@@ -96,9 +96,6 @@
     return min(-(-PAIR_ROWS * (pair + 1) // LANE) * LANE, ROWS_DEV)
 
 
-PIECES = (0, 2, 5)
-
-
 def legendre_kernel(
     me_ref, owner_hbm, lat_owner_hbm, table_ref, spectral_hbm, out_ref, owner, lat_owner, table, spectral, four, small, large
 ):
@@ -106,12 +103,8 @@
         pltpu.make_async_copy(owner_hbm, owner, small.at[0]),
         pltpu.make_async_copy(lat_owner_hbm, lat_owner, small.at[1]),
     ]
-    pieces = {}
-    for index, (pair, end) in enumerate(zip(PIECES, PIECES[1:] + (PAIRS_DEV,))):
-        start = last_row(pair - 1) if pair else 0
-        at = pl.ds(start, last_row(end - 1) - start)
-        pieces[pair] = pltpu.make_async_copy(spectral_hbm.at[at], spectral.at[at], large.at[index])
-    for copy in copies + list(pieces.values()):
+    whole = pltpu.make_async_copy(spectral_hbm, spectral, large.at[0])
+    for copy in [whole] + copies:
         copy.start()
     for index in range(8):
         table[4 * index : 4 * index + 4, 0:ROWS_DEV] = table_ref[index].astype(f32)
@@ -135,8 +128,8 @@
         left = jnp.concatenate(
             [block * mask.astype(bf16) for mask in (even, even * even_sign, odd, odd * odd_sign)], axis=0
         )
-        if pair in pieces:
-            pieces[pair].wait()
+        if pair == 0:
+            whole.wait()
         values = jnp.dot(left, spectral[start:stop, :], preferred_element_type=f32)
         four[2 * pair * NLAT : 2 * (pair + 1) * NLAT, :] = values
         if pair % 2 == 1:
@@ -367,7 +360,7 @@
             pltpu.VMEM((ROWS_DEV, COLS), bf16),
             pltpu.VMEM((SLOTS * NLAT, COLS), f32),
             dma((2,)),
-            dma((len(PIECES),)),
+            dma((1,)),
         ],
         compiler_params=params(24),
         name="legendre",

time: 53.6 us -> 54.1 us (level)
  no operation moved by 1% of the time
where the time goes in v5:
time: 54.1 us; the launch traced here: 53.8 us
  blocking collectives  17 us (31%)
  starting transfers between devices  13.4 us (25%)
  Pallas kernels  12.7 us (23%)
  waiting for transfers between devices  10.6 us (20%)
    all_gather x1, blocking collectives, per_device(): tables = lax.all_gather(table, 'lev', axis=0, tiled=False)  17 us
    all_to_all x1, starting transfers between devices, per_device(): lax.all_to_all(four, 'wave', split_axis=0, concat_axis=0, tiled=True)  13.4 us
    all_to_all x1, waiting for transfers between devices, per_device(): lax.all_to_all(four, 'wave', split_axis=0, concat_axis=0, tiled=True)  10.6 us
    pallas_call x1, Pallas kernels, per_device(): pl.pallas_call(basis_kernel, out_shape=(pltpu.VMEM(near_shape, bf16), plt...  5.6 us
    pallas_call x1, Pallas kernels, per_device(): pl.pallas_call(legendre_kernel, out_shape=jax.ShapeDtypeStruct((N_WAVE, S...  4.13 us
    pallas_call x1, Pallas kernels, per_device(): pl.pallas_call(fourier_kernel, out_shape=pltpu.HBM((1, LEVELS, NLON_PAD),...  3 us
  transfers between devices with their start and end apart: 1, of which 1 were waited for; matrix products, arithmetic and copies ran while one was open for 0% of the time, Pallas kernels for 10%

profile of v5, /device:TPU:2, one launch (start us, length us, event | category | flops | bytes accessed | tf_op | source)
XLA Modules:
  0.0 53.8 jit_solution(9703753529298412808)
XLA Ops:
  0.0 17.0 %all-gather.1.table_ref = bf16[8,4,12820]{2,1,0:T(4,128)(2,1)S(1)} all-gather(bf16[1,4,12820]{2,1,0:T(4,128)(2,1)} %bitcast.2), channel_id=2, replica_groups=mesh['wave'=64,'lev'=8] {'lev'}, dimensions={0}, use_global_device_ids=true | all-gather | bytes 923040 | tf_op jit(solution)/shard_map/all_gather | solution.py:342
  17.0 4.1 %legendre.1.after_hbm = bf16[64,5,4,128]{3,2,1,0:T(4,128)(2,1)} custom-call(s32[1]{0:T(128)} %bitcast.me_ref, s32[1280]{0:T(1024)} %owner_hbm.3, s32[64]{0:T(128)} %lat_owner_hbm.5, bf16[8,4,12820]{2,1,0:T(4,128)(2,1)S(1)} %all-gather.1.table_ref, bf16[12820,128]{1,0:T(8,128)(2,1)} %spectral_hbm.1), custom_call_target="tpu_custom_call" | custom-call | tf_op jit(solution)/shard_map/legendre/pallas_call | solution.py:351
  21.2 13.4 %all-to-all-start = ((bf16[64,5,4,128]{3,2,1,0:T(4,128)(2,1)}), bf16[64,5,4,128]{3,2,1,0:T(4,128)(2,1)S(1)}, u32[]{:S(2)}, u32[]{:S(2)}) async-start(bf16[64,5,4,128]{3,2,1,0:T(4,128)(2,1)} %legendre.1.after_hbm), calls=%async_computation | async-start | bytes 655360 | tf_op jit(solution)/shard_map/all_to_all | solution.py:368
  34.5 5.6 %basis.1 = (bf16[4,2,1280,128]{3,2,1,0:T(8,128)(2,1)S(1)}, bf16[2,2,1280,128]{3,2,1,0:T(8,128)(2,1)}, f32[8,640]{1,0:T(8,128)S(1)}) custom-call(s32[1]{0:T(128)} %bitcast.me_ref, s32[1280]{0:T(1024)} %owner_hbm.3, s32[64]{0:T(128)} %lat_owner_hbm.5, s32[32]{0:T(128)} %lat_points_hbm.3, bf16[64,5,4,128]{3,2,1,0:T(4,128)(2,1)} %legendre.1.after_hbm), custom_call_target="tpu_custom_call" | custom-call | tf_op jit(solution)/shard_map/basis/pallas_call | solution.py:371
  40.1 10.6 %all-to-all-done.received_ref = bf16[64,5,4,128]{3,2,1,0:T(4,128)(2,1)S(1)} async-done(((bf16[64,5,4,128]{3,2,1,0:T(4,128)(2,1)}), bf16[64,5,4,128]{3,2,1,0:T(4,128)(2,1)S(1)}, u32[]{:S(2)}, u32[]{:S(2)}) %all-to-all-start) | async-done | bytes 327712 | tf_op jit(solution)/shard_map/all_to_all | solution.py:368
  50.8 3.0 %fourier.1 = bf16[1,64,5376]{2,1,0:T(8,128)(2,1)} custom-call(s32[1]{0:T(128)} %bitcast.me_ref, s32[64]{0:T(128)} %lat_owner_hbm.5, s32[32]{0:T(128)} %lat_points_hbm.3, bf16[64,5,4,128]{3,2,1,0:T(4,128)(2,1)S(1)} %all-to-all-done.received_ref, f32[8,640]{1,0:T(8,128)S(1)} %get-tuple-element.8.scale, bf16[4,2,1280,128]{3,2,1,0:T(8,128)(2,1)S(1)} %get-tuple-element.9.near, ...), custom_call_target="tpu_custom_call" | custom-call | tf_op jit(solution)/shard_map/fourier/pallas_call | solution.py:388
Async XLA Ops:
  21.2 29.6 %all-to-all-start = ((bf16[64,5,4,128]{3,2,1,0:T(4,128)(2,1)}), bf16[64,5,4,128]{3,2,1,0:T(4,128)(2,1)S(1)}, u32[]{:S(2)}, u32[]{:S(2)}) async-start(bf16[64,5,4,128]{3,2,1,0:T(4,128)(2,1)} %legendre.1.after_hbm), calls=%async_computation | async-start | bytes 655360 | tf_op jit(solution)/shard_map/all_to_all | solution.py:368

commit v6 on v4

--- a/solution.py
+++ b/solution.py
@@ -100,7 +100,8 @@
 
 
 def legendre_kernel(
-    me_ref, owner_hbm, lat_owner_hbm, table_ref, spectral_hbm, out_ref, owner, lat_owner, table, spectral, four, small, large
+    me_ref, owner_hbm, lat_owner_hbm, table_ref, spectral_hbm, out_hbm,
+    owner, lat_owner, table, spectral, four, parts, small, large, leave,
 ):
     copies = [
         pltpu.make_async_copy(owner_hbm, owner, small.at[0]),
@@ -118,6 +119,7 @@
     for copy in copies:
         copy.wait()
     locals_ = local_pairs(owner_rows(owner), me_ref[0].astype(f32))
+    outs = []
     for pair in range(PAIRS_DEV):
         start, stop = first_row(pair), last_row(pair)
         width = stop - start
@@ -143,7 +145,11 @@
             part = pair // 2
             for latitude in range(NLAT):
                 rows = four[pl.ds(4 * part * NLAT + latitude, 4, stride=NLAT), :]
-                out_ref[lat_owner[latitude], part] = rows.astype(bf16)
+                parts[part, lat_owner[latitude]] = rows.astype(bf16)
+            outs.append(pltpu.make_async_copy(parts.at[part], out_hbm.at[:, part], leave.at[part]))
+            outs[-1].start()
+    for copy in outs:
+        copy.wait()
 
 
 def circle(quarters_per_turn, numerator, inverse):
@@ -357,17 +363,19 @@
     dma = pltpu.SemaphoreType.DMA
     four = pl.pallas_call(
         legendre_kernel,
-        out_shape=jax.ShapeDtypeStruct((N_WAVE, SLOTS // 4, 4, COLS), bf16),
+        out_shape=pltpu.HBM((N_WAVE, SLOTS // 4, 4, COLS), bf16),
         in_specs=[SMEM, HBM, HBM, VMEM, HBM],
-        out_specs=VMEM,
+        out_specs=HBM,
         scratch_shapes=[
             owner_scratch,
             lat_owner_scratch,
             pltpu.VMEM((NORTH, ROWS_PAD), f32),
             pltpu.VMEM((ROWS_DEV, COLS), bf16),
             pltpu.VMEM((SLOTS * NLAT, COLS), f32),
+            pltpu.VMEM((SLOTS // 4, N_WAVE, 4, COLS), bf16),
             dma((2,)),
             dma((len(PIECES),)),
+            dma((SLOTS // 4,)),
         ],
         compiler_params=params(24),
         name="legendre",

time: 53.6 us -> 53.6 us (level)
  no operation moved by 1% of the time
where the time goes in v6:
time: 53.6 us; the launch traced here: 53.3 us
  blocking collectives  17 us (32%)
  starting transfers between devices  13.4 us (25%)
  Pallas kernels  12.3 us (23%)
  waiting for transfers between devices  10.6 us (20%)
    all_gather x1, blocking collectives, per_device(): tables = lax.all_gather(table, 'lev', axis=0, tiled=False)  17 us
    all_to_all x1, starting transfers between devices, per_device(): lax.all_to_all(four, 'wave', split_axis=0, concat_axis=0, tiled=True)  13.4 us
    all_to_all x1, waiting for transfers between devices, per_device(): lax.all_to_all(four, 'wave', split_axis=0, concat_axis=0, tiled=True)  10.6 us
    pallas_call x1, Pallas kernels, per_device(): pl.pallas_call(basis_kernel, out_shape=(pltpu.VMEM(near_shape, bf16), plt...  5.6 us
    pallas_call x1, Pallas kernels, per_device(): pl.pallas_call(legendre_kernel, out_shape=pltpu.HBM((N_WAVE, SLOTS // 4,...  3.67 us
    pallas_call x1, Pallas kernels, per_device(): pl.pallas_call(fourier_kernel, out_shape=pltpu.HBM((1, LEVELS, NLON_PAD),...  3 us
  transfers between devices with their start and end apart: 1, of which 1 were waited for; matrix products, arithmetic and copies ran while one was open for 0% of the time, Pallas kernels for 10%

profile of v6, /device:TPU:2, one launch (start us, length us, event | category | flops | bytes accessed | tf_op | source)
XLA Modules:
  0.0 53.3 jit_solution(15953764113309042608)
XLA Ops:
  0.0 17.0 %all-gather.1.table_ref = bf16[8,4,12820]{2,1,0:T(4,128)(2,1)S(1)} all-gather(bf16[1,4,12820]{2,1,0:T(4,128)(2,1)} %bitcast.2), channel_id=2, replica_groups=mesh['wave'=64,'lev'=8] {'lev'}, dimensions={0}, use_global_device_ids=true | all-gather | bytes 923040 | tf_op jit(solution)/shard_map/all_gather | solution.py:355
  17.0 3.7 %legendre.1.after_hbm = bf16[64,5,4,128]{3,2,1,0:T(4,128)(2,1)} custom-call(s32[1]{0:T(128)} %bitcast.me_ref, s32[1280]{0:T(1024)} %owner_hbm.3, s32[64]{0:T(128)} %lat_owner_hbm.5, bf16[8,4,12820]{2,1,0:T(4,128)(2,1)S(1)} %all-gather.1.table_ref, bf16[12820,128]{1,0:T(8,128)(2,1)} %spectral_hbm.1), custom_call_target="tpu_custom_call" | custom-call | tf_op jit(solution)/shard_map/legendre/pallas_call | solution.py:364
  20.7 13.4 %all-to-all-start = ((bf16[64,5,4,128]{3,2,1,0:T(4,128)(2,1)}), bf16[64,5,4,128]{3,2,1,0:T(4,128)(2,1)S(1)}, u32[]{:S(2)}, u32[]{:S(2)}) async-start(bf16[64,5,4,128]{3,2,1,0:T(4,128)(2,1)} %legendre.1.after_hbm), calls=%async_computation | async-start | bytes 655360 | tf_op jit(solution)/shard_map/all_to_all | solution.py:383
  34.1 5.6 %basis.1 = (bf16[4,2,1280,128]{3,2,1,0:T(8,128)(2,1)S(1)}, bf16[2,2,1280,128]{3,2,1,0:T(8,128)(2,1)}, f32[8,640]{1,0:T(8,128)S(1)}) custom-call(s32[1]{0:T(128)} %bitcast.me_ref, s32[1280]{0:T(1024)} %owner_hbm.3, s32[64]{0:T(128)} %lat_owner_hbm.5, s32[32]{0:T(128)} %lat_points_hbm.3, bf16[64,5,4,128]{3,2,1,0:T(4,128)(2,1)} %legendre.1.after_hbm), custom_call_target="tpu_custom_call" | custom-call | tf_op jit(solution)/shard_map/basis/pallas_call | solution.py:386
  39.7 10.6 %all-to-all-done.received_ref = bf16[64,5,4,128]{3,2,1,0:T(4,128)(2,1)S(1)} async-done(((bf16[64,5,4,128]{3,2,1,0:T(4,128)(2,1)}), bf16[64,5,4,128]{3,2,1,0:T(4,128)(2,1)S(1)}, u32[]{:S(2)}, u32[]{:S(2)}) %all-to-all-start) | async-done | bytes 327712 | tf_op jit(solution)/shard_map/all_to_all | solution.py:383
  50.3 3.0 %fourier.1 = bf16[1,64,5376]{2,1,0:T(8,128)(2,1)} custom-call(s32[1]{0:T(128)} %bitcast.me_ref, s32[64]{0:T(128)} %lat_owner_hbm.5, s32[32]{0:T(128)} %lat_points_hbm.3, bf16[64,5,4,128]{3,2,1,0:T(4,128)(2,1)S(1)} %all-to-all-done.received_ref, f32[8,640]{1,0:T(8,128)S(1)} %get-tuple-element.8.scale, bf16[4,2,1280,128]{3,2,1,0:T(8,128)(2,1)S(1)} %get-tuple-element.9.near, ...), custom_call_target="tpu_custom_call" | custom-call | tf_op jit(solution)/shard_map/fourier/pallas_call | solution.py:403
Async XLA Ops:
  20.7 29.6 %all-to-all-start = ((bf16[64,5,4,128]{3,2,1,0:T(4,128)(2,1)}), bf16[64,5,4,128]{3,2,1,0:T(4,128)(2,1)S(1)}, u32[]{:S(2)}, u32[]{:S(2)}) async-start(bf16[64,5,4,128]{3,2,1,0:T(4,128)(2,1)} %legendre.1.after_hbm), calls=%async_computation | async-start | bytes 655360 | tf_op jit(solution)/shard_map/all_to_all | solution.py:383
